TPU v7x, 128 devices: a whole 4x4x4 slice. The times are simulated.
128 devices in a mesh: ctx: 16 (over y, x_lo, core), tp: 8 (over z, x_hi).
Axes of the slice: x: 4 (x_hi: 2, x_lo: 2; x = x_hi * 2 + x_lo), y: 4, z: 4, core: 2. Of those that a mesh axis runs over, the one named last changes fastest.
Arguments:
- gate_input: bfloat16 [4096, 8192], P('ctx', 'tp'), may hold values from -6 to 6
- value_input: bfloat16 [4096, 8192], P('ctx', 'tp'), may hold values from -6 to 6
- filter_taps: float32 [4096, 8192], P('ctx', 'tp'), may hold values from -1 to 1
- skip_gain: float32 [8192], P('tp'), may hold values from 0.3 to 3
- queries: bfloat16 [4096, 8192], P('ctx', 'tp'), may hold values from -8 to 8
- keys: bfloat16 [4096, 8192], P('ctx', 'tp'), may hold values from -8 to 8
Outputs:
- mixed: bfloat16 [4096, 8192], P('ctx', 'tp')
- attended: bfloat16 [4096, 8192], P('ctx', 'tp')
All inputs are finite; a program needn't handle non-finite values.
Results may differ from a plain program's by a relative error of at most 0.012.
Values may be sent and summed in bfloat16 or wider, within the bound.
No kernel may reach another device: no remote copies, remote signals or barrier semaphores. Data moves between devices by JAX's collectives and lax.ppermute only.
A program may use at most 128 MiB of HBM per device.

v0:
```python
import math

import numpy as np

import jax
import jax.numpy as jnp
from jax import lax
from jax.experimental import pallas as pl
from jax.experimental.pallas import tpu as pltpu
from jax.sharding import Mesh, PartitionSpec as P

HEAD_DIM = 128
CORES = 2
SCALE = 1.0 / math.sqrt(HEAD_DIM)
MASKED = -1e30
VMEM_LIMIT = 56 * 1024 * 1024


def transform_tables(rows):
    period = 2 * rows
    freq = np.arange(rows, dtype=np.float64)[:, None] + 0.5
    time = np.arange(period, dtype=np.float64)[None, :]
    angle = 2.0 * np.pi * freq * time / period
    forward = np.concatenate([np.cos(angle), -np.sin(angle)], axis=0)
    later = angle[:, rows:].T
    inverse = np.concatenate([np.cos(later), -np.sin(later)], axis=1) / rows
    return jnp.asarray(forward, jnp.bfloat16), jnp.asarray(inverse, jnp.bfloat16)


def pack_kernel(values_ref, taps_ref, out_ref):
    out_ref[0, 0] = values_ref[...]
    out_ref[0, 1] = taps_ref[...].astype(jnp.bfloat16)


def pack(values, taps):
    rows, channels = values.shape
    chips = channels // HEAD_DIM
    block = pl.BlockSpec((rows, HEAD_DIM), lambda p: (0, p))
    return pl.pallas_call(
        pack_kernel,
        grid=(chips,),
        in_specs=[block, block],
        out_specs=pl.BlockSpec((1, 2, rows, HEAD_DIM), lambda p: (p, 0, 0, 0)),
        out_shape=jax.ShapeDtypeStruct((chips, 2, rows, HEAD_DIM), jnp.bfloat16),
    )(values, taps)


def conv_kernel(
    core_ref,
    own_ref,
    other_ref,
    gate_ref,
    skip_ref,
    forward_ref,
    inverse_ref,
    out_ref,
    taps_all,
    x_spec,
    h_spec,
    y_spec,
):
    core = core_ref[0]
    blocks, _, rows, lanes = own_ref.shape

    def dot(a, b):
        return jnp.dot(a, b, preferred_element_type=jnp.float32)

    taps_all[0] = jnp.zeros((rows, lanes), jnp.bfloat16)
    taps_all[1] = jnp.zeros((rows, lanes), jnp.bfloat16)

    @pl.loop(0, blocks)
    def _(m):
        taps_all[2 * m + 2 + core] = own_ref[m, 1]
        taps_all[2 * m + 3 - core] = other_ref[m, 1]

    half = forward_ref[:, :rows]

    @pl.loop(0, blocks)
    def _(m):
        pair = jnp.concatenate([own_ref[m, 0], other_ref[m, 0]], axis=1)
        spectrum = dot(half, pair)
        x_spec[2 * m] = spectrum[:, :lanes]
        x_spec[2 * m + 1] = spectrum[:, lanes:]
        first = jnp.concatenate([taps_all[2 * m + 1], taps_all[2 * m + 2 * core]], axis=1)
        second = jnp.concatenate([taps_all[2 * m + 2], taps_all[2 * m + 2 * core + 1]], axis=1)
        spectrum = dot(forward_ref[...], jnp.concatenate([first, second], axis=0))
        h_spec[2 * m] = spectrum[:, :lanes]
        h_spec[2 * m + 1] = spectrum[:, lanes:]

    step = 8

    @pl.loop(0, rows // step)
    def _(t):
        re = pl.ds(pl.multiple_of(t * step, step), step)
        im = pl.ds(pl.multiple_of(rows + t * step, step), step)
        xr = [x_spec[j, re] for j in range(2 * blocks)]
        xi = [x_spec[j, im] for j in range(2 * blocks)]
        yr = [None] * blocks
        yi = [None] * blocks
        for lag in range(blocks):
            for side in range(2):
                hr = h_spec[2 * lag + side, re]
                hi = h_spec[2 * lag + side, im]
                for j in range(blocks - lag):
                    b = j + lag
                    ar, ai = xr[2 * j + side], xi[2 * j + side]
                    pr = ar * hr - ai * hi
                    pi = ar * hi + ai * hr
                    yr[b] = pr if yr[b] is None else yr[b] + pr
                    yi[b] = pi if yi[b] is None else yi[b] + pi
        for b in range(blocks):
            y_spec[b, re] = yr[b]
            y_spec[b, im] = yi[b]

    skip = skip_ref[...]

    @pl.loop(0, blocks // 2)
    def _(m):
        spectrum = jnp.concatenate([y_spec[2 * m], y_spec[2 * m + 1]], axis=1)
        convolved = dot(inverse_ref[...], spectrum.astype(jnp.bfloat16))
        for s in range(2):
            b = 2 * m + s
            part = convolved[:, s * lanes : (s + 1) * lanes]
            values = own_ref[b, 0].astype(jnp.float32)
            gated = gate_ref[b].astype(jnp.float32) * (part + skip * values)
            out_ref[b] = gated.astype(jnp.bfloat16)


def convolve(core, own, other, gate, skip):
    blocks, _, rows, lanes = own.shape
    forward, inverse = transform_tables(rows)
    vmem = pl.BlockSpec(memory_space=pltpu.VMEM)
    return pl.pallas_call(
        conv_kernel,
        in_specs=[pl.BlockSpec(memory_space=pltpu.SMEM)] + [vmem] * 6,
        out_specs=vmem,
        out_shape=jax.ShapeDtypeStruct((blocks, rows, lanes), jnp.bfloat16),
        scratch_shapes=[
            pltpu.VMEM((2 * blocks + 2, rows, lanes), jnp.bfloat16),
            pltpu.VMEM((2 * blocks, 2 * rows, lanes), jnp.float32),
            pltpu.VMEM((2 * blocks, 2 * rows, lanes), jnp.float32),
            pltpu.VMEM((blocks, 2 * rows, lanes), jnp.float32),
        ],
        compiler_params=pltpu.CompilerParams(vmem_limit_bytes=VMEM_LIMIT),
    )(core, own, other, gate, skip, forward, inverse)


def attend_kernel(core_ref, q_ref, ko_ref, kp_ref, vo_ref, vp_ref, out_ref):
    core = core_ref[0]
    blocks, rows, lanes = q_ref.shape
    row = lax.broadcasted_iota(jnp.int32, (rows, rows), 0)
    col = lax.broadcasted_iota(jnp.int32, (rows, rows), 1)
    on_diagonal = col <= row
    beside = jnp.full((rows, rows), core, jnp.int32) > 0

    def scores(q, k):
        return lax.dot_general(q, k, (((1,), (1,)), ((), ())), preferred_element_type=jnp.float32)

    for b in range(blocks):
        q = q_ref[b]
        parts = []
        for j in range(b + 1):
            so = scores(q, ko_ref[j]) * SCALE
            sp = scores(q, kp_ref[j]) * SCALE
            if j == b:
                so = jnp.where(on_diagonal, so, MASKED)
                sp = jnp.where(beside, sp, MASKED)
            parts += [so, sp]
        top = parts[0]
        for s in parts[1:]:
            top = jnp.maximum(top, s)
        top = jnp.max(top, axis=1, keepdims=True)
        total = None
        acc = None
        for j in range(b + 1):
            for side, v_ref in enumerate((vo_ref, vp_ref)):
                w = jnp.exp(parts[2 * j + side] - top)
                total = w if total is None else total + w
                pv = jnp.dot(w.astype(jnp.bfloat16), v_ref[j], preferred_element_type=jnp.float32)
                acc = pv if acc is None else acc + pv
        total = jnp.sum(total, axis=1, keepdims=True)
        out_ref[b] = (acc / total).astype(jnp.bfloat16)


def attend(core, q, k_own, k_other, v_own, v_other):
    vmem = pl.BlockSpec(memory_space=pltpu.VMEM)
    return pl.pallas_call(
        attend_kernel,
        in_specs=[pl.BlockSpec(memory_space=pltpu.SMEM)] + [vmem] * 5,
        out_specs=vmem,
        out_shape=jax.ShapeDtypeStruct(q.shape, jnp.bfloat16),
        compiler_params=pltpu.CompilerParams(vmem_limit_bytes=VMEM_LIMIT),
    )(core, q, k_own, k_other, v_own, v_other)


def to_heads(array):
    rows, channels = array.shape
    split = array.reshape(rows, channels // HEAD_DIM, HEAD_DIM).transpose(1, 0, 2)
    return lax.all_to_all(split, "chip", split_axis=0, concat_axis=0, tiled=True)


def to_positions(array):
    chips, rows, lanes = array.shape
    moved = lax.all_to_all(array, "chip", split_axis=0, concat_axis=0, tiled=True)
    return moved.transpose(1, 0, 2).reshape(rows, chips * lanes)


def swap(array):
    return lax.ppermute(array, "core", [(0, 1), (1, 0)])


def per_device(gate_input, value_input, filter_taps, skip_gain, queries, keys):
    chip = lax.axis_index("chip")
    core = lax.axis_index("core").astype(jnp.int32).reshape(1)
    own = lax.all_to_all(
        pack(value_input, filter_taps), "chip", split_axis=0, concat_axis=0, tiled=True
    )
    other = swap(own)
    gate = to_heads(gate_input)
    q = to_heads(queries)
    k_own = to_heads(keys)
    k_other = swap(k_own)
    skip = lax.dynamic_slice(skip_gain, (chip * HEAD_DIM,), (HEAD_DIM,)).reshape(1, HEAD_DIM)
    v_own = convolve(core, own, other, gate, skip)
    v_other = swap(v_own)
    mixed = to_positions(v_own)
    attended = to_positions(attend(core, q, k_own, k_other, v_own, v_other))
    return (mixed, attended)


def solution(mesh):
    ctx, tp = mesh.devices.shape
    fine = Mesh(mesh.devices.reshape(ctx // CORES, CORES, tp), ("chip", "core", "tp"))
    rows = P(("chip", "core"), "tp")
    return jax.shard_map(
        per_device,
        mesh=fine,
        in_specs=(rows, rows, rows, P("tp"), rows, rows),
        out_specs=(rows, rows),
        check_vma=False,
    )
```

profile of v0, /device:TPU:1, one launch (start us, length us, event | category | flops | bytes accessed | tf_op | source)
XLA Modules:
  0.0 102.5 jit_solution(6692341812481384806)
XLA Ops:
  0.6 0.0 copy-start
  0.6 5.3 %shard_map.95 = bf16[8,2,256,128]{3,2,1,0:T(8,128)(2,1)} custom-call(bf16[256,1024]{1,0:T(8,128)(2,1)} %values_ref.1, f32[256,1024]{1,0:T(8,128)} %taps_ref.1), custom_call_target="tpu_custom_call" | custom-call | tf_op jit(solution)/shard_map/pallas_call | solution.py:39
  6.0 0.0 copy-start.6
  6.0 6.1 %all-to-all-start = ((bf16[8,2,256,128]{3,2,1,0:T(8,128)(2,1)}), bf16[8,2,256,128]{3,2,1,0:T(8,128)(2,1)S(1)}, u32[]{:S(2)}, u32[]{:S(2)}) async-start(bf16[8,2,256,128]{3,2,1,0:T(8,128)(2,1)} %shard_map.95), calls=%async_computation | async-start | bytes 2097152 | tf_op jit(solution)/shard_map/all_to_all | solution.py:215
  12.1 0.0 copy-done.6
  12.1 0.2 copy.10
  12.3 1.0 copy.11
  13.3 13.3 %all-to-all-done.own_ref = bf16[8,2,256,128]{3,2,1,0:T(8,128)(2,1)S(1)} async-done(((bf16[8,2,256,128]{3,2,1,0:T(8,128)(2,1)}), bf16[8,2,256,128]{3,2,1,0:T(8,128)(2,1)S(1)}, u32[]{:S(2)}, u32[]{:S(2)}) %all-to-all-start) | async-done | bytes 1048608 | tf_op jit(solution)/shard_map/all_to_all | solution.py:215
  26.6 0.0 copy-start.1
  26.6 4.1 %all-to-all-start.1 = ((bf16[8,256,128]{2,1,0:T(8,128)(2,1)}), bf16[8,256,128]{2,1,0:T(8,128)(2,1)S(1)}, u32[]{:S(2)}, u32[]{:S(2)}) async-start(bf16[8,256,128]{2,1,0:T(8,128)(2,1)} %bitcast.2), calls=%async_computation.1 | async-start | bytes 1048576 | tf_op jit(solution)/shard_map/all_to_all | solution.py:199
  30.7 1.6 %collective-permute-start = (bf16[8,2,256,128]{3,2,1,0:T(8,128)(2,1)S(1)}, bf16[8,2,256,128]{3,2,1,0:T(8,128)(2,1)S(1)}, u32[]{:S(2)}, u32[]{:S(2)}) collective-permute-start(bf16[8,2,256,128]{3,2,1,0:T(8,128)(2,1)S(1)} %all-to-all-done.own_ref), channel_id=1, source_target_pairs={{0,8},{8,0},{1,9},{9,1},{2,10},{10,2},{3,11},{11,3},{4,12},{12,4},... | collective-permute-start | bytes 3145736 | tf_op jit(solution)/shard_map/ppermute | solution.py:209
  32.3 1.2 %copy.15 = bf16[256,1024]{0,1:T(8,128)(2,1)S(1)} copy(bf16[256,1024]{1,0:T(8,128)(2,1)} %param.13) | data formatting | bytes 1048576 | tf_op args[5]
  33.6 0.0 copy-done.1
  33.6 1.0 copy.16
  34.6 4.8 %all-to-all-done.1.gate_ref = bf16[8,256,128]{2,1,0:T(8,128)(2,1)S(1)} async-done(((bf16[8,256,128]{2,1,0:T(8,128)(2,1)}), bf16[8,256,128]{2,1,0:T(8,128)(2,1)S(1)}, u32[]{:S(2)}, u32[]{:S(2)}) %all-to-all-start.1) | async-done | bytes 524320 | tf_op jit(solution)/shard_map/all_to_all | solution.py:199
  39.3 0.0 copy-start.2
  39.3 0.8 copy-done.2
  40.1 3.5 %all-to-all-start.4 = ((bf16[8,256,128]{2,1,0:T(8,128)(2,1)}), bf16[8,256,128]{2,1,0:T(8,128)(2,1)S(1)}, u32[]{:S(2)}, u32[]{:S(2)}) async-start(bf16[8,256,128]{2,1,0:T(8,128)(2,1)} %bitcast.9), calls=%async_computation.4 | async-start | bytes 1048576 | tf_op jit(solution)/shard_map/all_to_all | solution.py:199
  43.6 1.2 %copy.13 = bf16[256,1024]{0,1:T(8,128)(2,1)S(1)} copy(bf16[256,1024]{1,0:T(8,128)(2,1)} %param.12) | data formatting | bytes 1048576 | tf_op args[4]
  44.9 1.0 copy.14
  45.9 5.3 %all-to-all-done.4.ko_ref = bf16[8,256,128]{2,1,0:T(8,128)(2,1)S(1)} async-done(((bf16[8,256,128]{2,1,0:T(8,128)(2,1)}), bf16[8,256,128]{2,1,0:T(8,128)(2,1)S(1)}, u32[]{:S(2)}, u32[]{:S(2)}) %all-to-all-start.4) | async-done | bytes 524320 | tf_op jit(solution)/shard_map/all_to_all | solution.py:199
  51.2 0.0 copy-start.3
  51.2 3.5 %all-to-all-start.3 = ((bf16[8,256,128]{2,1,0:T(8,128)(2,1)}), bf16[8,256,128]{2,1,0:T(8,128)(2,1)S(1)}, u32[]{:S(2)}, u32[]{:S(2)}) async-start(bf16[8,256,128]{2,1,0:T(8,128)(2,1)} %bitcast.7), calls=%async_computation.3 | async-start | bytes 1048576 | tf_op jit(solution)/shard_map/all_to_all | solution.py:199
  54.7 0.0 copy-done
  54.7 0.7 dynamic-slice_bitcast_fusion.skip_ref
  55.4 0.0 copy-done.3
  55.4 3.5 %collective-permute-start.1 = (bf16[8,256,128]{2,1,0:T(8,128)(2,1)S(1)}, bf16[8,256,128]{2,1,0:T(8,128)(2,1)}, u32[]{:S(2)}, u32[]{:S(2)}) collective-permute-start(bf16[8,256,128]{2,1,0:T(8,128)(2,1)S(1)} %all-to-all-done.4.ko_ref), channel_id=1, source_target_pairs={{0,8},{8,0},{1,9},{9,1},{2,10},{10,2},{3,11},{11,3},{4,12},{12,4},... | collective-permute-start | bytes 1572872 | tf_op jit(solution)/shard_map/ppermute | solution.py:209
  58.9 0.0 collective-permute-done.other_ref
  58.9 0.0 copy-start.5
  58.9 1.0 copy-done.5
  59.9 9.8 %shard_map.96.vo_ref = bf16[8,256,128]{2,1,0:T(8,128)(2,1)} custom-call(s32[1]{0:T(128)} %bitcast.core_ref, bf16[8,2,256,128]{3,2,1,0:T(8,128)(2,1)} %copy-done.1, bf16[8,2,256,128]{3,2,1,0:T(8,128)(2,1)} %copy-done.5, bf16[8,256,128]{2,1,0:T(8,128)(2,1)} %copy-done.2, f32[1,128]{1,0:T(1,128)} %dynamic-slice_bitcast_fusion.skip_ref, ...), custom_call_target="tpu_custom_call" | custom-call | tf_op jit(solution)/shard_map/pallas_call | solution.py:133
  69.7 0.0 collective-permute-start.2
  69.7 0.0 all-to-all-done.3.q_ref
  69.7 0.0 copy-start.4
  69.7 0.8 copy-done.4
  70.5 5.3 %all-to-all-start.2 = ((bf16[8,256,128]{2,1,0:T(8,128)(2,1)}), bf16[8,256,128]{2,1,0:T(8,128)(2,1)S(1)}, u32[]{:S(2)}, u32[]{:S(2)}) async-start(bf16[8,256,128]{2,1,0:T(8,128)(2,1)} %shard_map.96.vo_ref), calls=%async_computation.2 | async-start | bytes 1048576 | tf_op jit(solution)/shard_map/all_to_all | solution.py:204
  75.8 0.0 collective-permute-done.1.kp_ref
  75.8 0.0 collective-permute-done.2.vp_ref
  75.8 0.0 copy-start.7
  75.8 0.8 copy-done.7
  76.6 10.7 %shard_map.97 = bf16[8,256,128]{2,1,0:T(8,128)(2,1)} custom-call(s32[1]{0:T(128)} %bitcast.core_ref, bf16[8,256,128]{2,1,0:T(8,128)(2,1)} %copy-done.4, bf16[8,256,128]{2,1,0:T(8,128)(2,1)} %copy-done.3, bf16[8,256,128]{2,1,0:T(8,128)(2,1)} %collective-permute-done.1.kp_ref, bf16[8,256,128]{2,1,0:T(8,128)(2,1)} %shard_map.96.vo_ref, ...), custom_call_target="tpu_custom_call" | custom-call | tf_op jit(solution)/shard_map/pallas_call | solution.py:187
  87.3 0.0 all-to-all-done.2
  87.3 5.1 %all-to-all-start.5 = ((bf16[8,256,128]{2,1,0:T(8,128)(2,1)}), bf16[8,256,128]{2,1,0:T(8,128)(2,1)S(1)}, u32[]{:S(2)}, u32[]{:S(2)}) async-start(bf16[8,256,128]{2,1,0:T(8,128)(2,1)} %shard_map.97), calls=%async_computation.5 | async-start | bytes 1048576 | tf_op jit(solution)/shard_map/all_to_all | solution.py:204
  92.5 0.2 copy.12
  92.7 1.0 copy.18
  93.7 7.5 %all-to-all-done.5 = bf16[8,256,128]{2,1,0:T(8,128)(2,1)S(1)} async-done(((bf16[8,256,128]{2,1,0:T(8,128)(2,1)}), bf16[8,256,128]{2,1,0:T(8,128)(2,1)S(1)}, u32[]{:S(2)}, u32[]{:S(2)}) %all-to-all-start.5) | async-done | bytes 524320 | tf_op jit(solution)/shard_map/all_to_all | solution.py:204
  101.3 0.2 copy.17
  101.5 1.0 copy.19
Async XLA Ops:
  0.6 54.1 %copy-start = (f32[1024]{0:T(1024)S(1)}, f32[1024]{0:T(1024)}, u32[]{:S(2)}) copy-start(f32[1024]{0:T(1024)} %param.11) | copy-start | bytes 12292
  6.0 6.1 %copy-start.6 = (bf16[256,1024]{1,0:T(8,128)(2,1)S(1)}, bf16[256,1024]{1,0:T(8,128)(2,1)}, u32[]{:S(2)}) copy-start(bf16[256,1024]{1,0:T(8,128)(2,1)} %param.8) | copy-start | bytes 1572868
  6.0 20.6 %all-to-all-start = ((bf16[8,2,256,128]{3,2,1,0:T(8,128)(2,1)}), bf16[8,2,256,128]{3,2,1,0:T(8,128)(2,1)S(1)}, u32[]{:S(2)}, u32[]{:S(2)}) async-start(bf16[8,2,256,128]{3,2,1,0:T(8,128)(2,1)} %shard_map.95), calls=%async_computation | async-start | bytes 2097152 | tf_op jit(solution)/shard_map/all_to_all | solution.py:215
  26.6 7.0 %copy-start.1 = (bf16[8,2,256,128]{3,2,1,0:T(8,128)(2,1)}, bf16[8,2,256,128]{3,2,1,0:T(8,128)(2,1)S(1)}, u32[]{:S(2)}) copy-start(bf16[8,2,256,128]{3,2,1,0:T(8,128)(2,1)S(1)} %all-to-all-done.own_ref) | copy-start | bytes 3145732
  26.6 12.8 %all-to-all-start.1 = ((bf16[8,256,128]{2,1,0:T(8,128)(2,1)}), bf16[8,256,128]{2,1,0:T(8,128)(2,1)S(1)}, u32[]{:S(2)}, u32[]{:S(2)}) async-start(bf16[8,256,128]{2,1,0:T(8,128)(2,1)} %bitcast.2), calls=%async_computation.1 | async-start | bytes 1048576 | tf_op jit(solution)/shard_map/all_to_all | solution.py:199
  30.7 28.2 %collective-permute-start = (bf16[8,2,256,128]{3,2,1,0:T(8,128)(2,1)S(1)}, bf16[8,2,256,128]{3,2,1,0:T(8,128)(2,1)S(1)}, u32[]{:S(2)}, u32[]{:S(2)}) collective-permute-start(bf16[8,2,256,128]{3,2,1,0:T(8,128)(2,1)S(1)} %all-to-all-done.own_ref), channel_id=1, source_target_pairs={{0,8},{8,0},{1,9},{9,1},{2,10},{10,2},{3,11},{11,3},{4,12},{12,4},... | collective-permute-start | bytes 3145736 | tf_op jit(solution)/shard_map/ppermute | solution.py:209
  39.3 0.8 copy-start.2
  40.1 11.1 %all-to-all-start.4 = ((bf16[8,256,128]{2,1,0:T(8,128)(2,1)}), bf16[8,256,128]{2,1,0:T(8,128)(2,1)S(1)}, u32[]{:S(2)}, u32[]{:S(2)}) async-start(bf16[8,256,128]{2,1,0:T(8,128)(2,1)} %bitcast.9), calls=%async_computation.4 | async-start | bytes 1048576 | tf_op jit(solution)/shard_map/all_to_all | solution.py:199
  51.2 4.2 %copy-start.3 = (bf16[8,256,128]{2,1,0:T(8,128)(2,1)}, bf16[8,256,128]{2,1,0:T(8,128)(2,1)S(1)}, u32[]{:S(2)}) copy-start(bf16[8,256,128]{2,1,0:T(8,128)(2,1)S(1)} %all-to-all-done.4.ko_ref) | copy-start | bytes 1572868
  51.2 18.4 %all-to-all-start.3 = ((bf16[8,256,128]{2,1,0:T(8,128)(2,1)}), bf16[8,256,128]{2,1,0:T(8,128)(2,1)S(1)}, u32[]{:S(2)}, u32[]{:S(2)}) async-start(bf16[8,256,128]{2,1,0:T(8,128)(2,1)} %bitcast.7), calls=%async_computation.3 | async-start | bytes 1048576 | tf_op jit(solution)/shard_map/all_to_all | solution.py:199
  55.4 20.4 %collective-permute-start.1 = (bf16[8,256,128]{2,1,0:T(8,128)(2,1)S(1)}, bf16[8,256,128]{2,1,0:T(8,128)(2,1)}, u32[]{:S(2)}, u32[]{:S(2)}) collective-permute-start(bf16[8,256,128]{2,1,0:T(8,128)(2,1)S(1)} %all-to-all-done.4.ko_ref), channel_id=1, source_target_pairs={{0,8},{8,0},{1,9},{9,1},{2,10},{10,2},{3,11},{11,3},{4,12},{12,4},... | collective-permute-start | bytes 1572872 | tf_op jit(solution)/shard_map/ppermute | solution.py:209
  58.9 1.0 copy-start.5
  69.7 6.1 %collective-permute-start.2 = (bf16[8,256,128]{2,1,0:T(8,128)(2,1)}, bf16[8,256,128]{2,1,0:T(8,128)(2,1)S(1)}, u32[]{:S(2)}, u32[]{:S(2)}) collective-permute-start(bf16[8,256,128]{2,1,0:T(8,128)(2,1)} %shard_map.96.vo_ref), channel_id=1, source_target_pairs={{0,8},{8,0},{1,9},{9,1},{2,10},{10,2},{3,11},{11,3},{4,12},{12,4},... | collective-permute-start | bytes 1572872 | tf_op jit(solution)/shard_map/ppermute | solution.py:209
  69.7 0.8 copy-start.4
  70.5 16.9 %all-to-all-start.2 = ((bf16[8,256,128]{2,1,0:T(8,128)(2,1)}), bf16[8,256,128]{2,1,0:T(8,128)(2,1)S(1)}, u32[]{:S(2)}, u32[]{:S(2)}) async-start(bf16[8,256,128]{2,1,0:T(8,128)(2,1)} %shard_map.96.vo_ref), calls=%async_computation.2 | async-start | bytes 1048576 | tf_op jit(solution)/shard_map/all_to_all | solution.py:204
  75.8 0.8 copy-start.7
  87.3 13.9 %all-to-all-start.5 = ((bf16[8,256,128]{2,1,0:T(8,128)(2,1)}), bf16[8,256,128]{2,1,0:T(8,128)(2,1)S(1)}, u32[]{:S(2)}, u32[]{:S(2)}) async-start(bf16[8,256,128]{2,1,0:T(8,128)(2,1)} %shard_map.97), calls=%async_computation.5 | async-start | bytes 1048576 | tf_op jit(solution)/shard_map/all_to_all | solution.py:204
where the time goes:
time: 104 us; the launch traced here: 102 us
  starting transfers between devices  32.8 us (32%)
  waiting for transfers between devices  30.9 us (30%)
  Pallas kernels  25.9 us (25%)
  local copies, waits for them, and re-layouts  12.2 us (12%)
    all_to_all x1, waiting for transfers between devices, per_device(): lax.all_to_all(pack(value_input, filter_taps), 'chip', split_axis=0, conc...  13.3 us
    all_to_all x3, starting transfers between devices, to_heads(): lax.all_to_all(split, 'chip', split_axis=0, concat_axis=0, tiled=True)  11.1 us
    pallas_call x1, Pallas kernels, attend(): pl.pallas_call(attend_kernel, in_specs=[pl.BlockSpec(memory_space=pltpu.S...  10.7 us
    all_to_all x2, starting transfers between devices, to_positions(): lax.all_to_all(array, 'chip', split_axis=0, concat_axis=0, tiled=True)  10.5 us
    all_to_all x3, waiting for transfers between devices, to_heads(): lax.all_to_all(split, 'chip', split_axis=0, concat_axis=0, tiled=True)  10.1 us
    pallas_call x1, Pallas kernels, convolve(): pl.pallas_call(conv_kernel, in_specs=[pl.BlockSpec(memory_space=pltpu.SME...  9.78 us
    unnamed x21, local copies, waits for them, and re-layouts  8.07 us
    all_to_all x2, waiting for transfers between devices, to_positions(): lax.all_to_all(array, 'chip', split_axis=0, concat_axis=0, tiled=True)  7.53 us
  transfers between devices with their start and end apart: 9, of which 4 were waited for; matrix products, arithmetic and copies ran while one was open for 7% of the time, Pallas kernels for 20%

commit v1 on v0

v1 whole, which is shorter than its diff:
```python
import functools
import math

import numpy as np

import jax
import jax.numpy as jnp
from jax import lax
from jax.experimental import pallas as pl
from jax.experimental.pallas import tpu as pltpu
from jax.sharding import Mesh, PartitionSpec as P

HEAD_DIM = 128
CORES = 2
SCALE = 1.0 / math.sqrt(HEAD_DIM)
MASKED = -1e30
TO_EXP2 = SCALE * math.log2(math.e)
MIB = 1024 * 1024


def transform_tables(rows):
    period = 2 * rows
    freq = np.arange(rows, dtype=np.float64)[:, None] + 0.5
    time = np.arange(period, dtype=np.float64)[None, :]
    angle = 2.0 * np.pi * freq * time / period
    forward = np.concatenate([np.cos(angle), -np.sin(angle)], axis=0)
    later = angle[:, rows:].T
    inverse = np.concatenate([np.cos(later), -np.sin(later)], axis=1) / rows
    return jnp.asarray(forward, jnp.bfloat16), jnp.asarray(inverse, jnp.bfloat16)


def room(mib, flops=0, moved=0):
    return dict(
        compiler_params=pltpu.CompilerParams(vmem_limit_bytes=mib * MIB),
        cost_estimate=pl.CostEstimate(flops=flops, bytes_accessed=moved, transcendentals=0),
    )


VMEM = pl.BlockSpec(memory_space=pltpu.VMEM)
SMEM = pl.BlockSpec(memory_space=pltpu.SMEM)
ANYWHERE = pl.BlockSpec(memory_space=pl.ANY)


def pack_kernel(*refs, count, parts):
    inputs, out, held, made, sems, out_sem = (
        refs[:count],
        refs[count],
        refs[count + 1 : 2 * count + 1],
        refs[-3],
        refs[-2],
        refs[-1],
    )
    size = inputs[0].shape[0] // parts
    copies = [
        [
            pltpu.make_async_copy(
                ref.at[pl.ds(s * size, size)], buf.at[pl.ds(s * size, size)], sems.at[i, s]
            )
            for i, (ref, buf) in enumerate(zip(inputs, held))
        ]
        for s in range(parts)
    ]
    for part in copies:
        for c in part:
            c.start()
    stores = []
    for s, part in enumerate(copies):
        span = slice(s * size, (s + 1) * size)
        for i, c in enumerate(part):
            c.wait()
            for p in range(out.shape[0]):
                lanes = slice(p * HEAD_DIM, (p + 1) * HEAD_DIM)
                made[p, i, span] = held[i][span, lanes].astype(jnp.bfloat16)
            rows = pl.ds(s * size, size)
            stores.append(
                pltpu.make_async_copy(made.at[:, i, rows], out.at[:, i, rows], out_sem.at[i, s])
            )
            stores[-1].start()
    for c in stores:
        c.wait()


def pack(*arrays):
    rows, channels = arrays[0].shape
    chips = channels // HEAD_DIM
    count = len(arrays)
    parts = 4
    shape = (chips, count, rows, HEAD_DIM)
    return pl.pallas_call(
        functools.partial(pack_kernel, count=count, parts=parts),
        in_specs=[ANYWHERE] * count,
        out_specs=ANYWHERE,
        out_shape=jax.ShapeDtypeStruct(shape, jnp.bfloat16),
        scratch_shapes=[pltpu.VMEM(a.shape, a.dtype) for a in arrays]
        + [pltpu.VMEM(shape, jnp.bfloat16)]
        + [pltpu.SemaphoreType.DMA((count, parts))] * 2,
        **room(56, 0, 6 * MIB),
    )(*arrays)


def pack_rest_kernel(queries, keys, forward, inverse, out, forward_out, inverse_out):
    for p in range(out.shape[0]):
        lanes = slice(p * HEAD_DIM, (p + 1) * HEAD_DIM)
        out[p, 0] = queries[:, lanes]
        out[p, 1] = keys[:, lanes]
    forward_out[...] = forward[...]
    inverse_out[...] = inverse[...]


def pack_rest(queries, keys):
    rows, channels = queries.shape
    chips = channels // HEAD_DIM
    tables = transform_tables(rows)
    out = jax.ShapeDtypeStruct((chips, 2, rows, HEAD_DIM), jnp.bfloat16)
    return pl.pallas_call(
        pack_rest_kernel,
        in_specs=[VMEM] * 4,
        out_specs=[VMEM] * 3,
        out_shape=[out] + [jax.ShapeDtypeStruct(t.shape, t.dtype) for t in tables],
        **room(16, 0, 6 * MIB),
    )(queries, keys, *tables)


def unpack_kernel(back, mixed, attended, sems):
    copies = []
    for p in range(back.shape[0]):
        lanes = pl.ds(p * HEAD_DIM, HEAD_DIM)
        for i, out in enumerate((mixed, attended)):
            copies.append(pltpu.make_async_copy(back.at[p, i], out.at[:, lanes], sems.at[i, p]))
    for c in copies:
        c.start()
    for c in copies:
        c.wait()


def unpack(back):
    chips, count, rows, lanes = back.shape
    out = jax.ShapeDtypeStruct((rows, chips * lanes), jnp.bfloat16)
    return pl.pallas_call(
        unpack_kernel,
        in_specs=[VMEM],
        out_specs=[ANYWHERE] * count,
        out_shape=[out] * count,
        scratch_shapes=[pltpu.SemaphoreType.DMA((count, chips))],
        **room(8, 0, 2 * MIB),
    )(back)


def conv_kernel(core_ref, own, other, skip_ref, forward, inverse, out_ref, taps, *specs):
    x_spec, h_spec, y_spec = specs
    blocks, _, rows, lanes = own.shape
    core = core_ref[0]

    def dot(a, b):
        return jnp.dot(a, b, preferred_element_type=jnp.float32)

    taps[0] = jnp.zeros((rows, lanes), jnp.bfloat16)
    taps[1] = jnp.zeros((rows, lanes), jnp.bfloat16)

    @pl.loop(0, blocks)
    def _(m):
        taps[2 * m + 2 + core] = own[m, 1]
        taps[2 * m + 3 - core] = other[m, 1]

    @pl.loop(0, blocks)
    def _(m):
        pair = jnp.concatenate([own[m, 0], other[m, 0]], axis=1)
        spectrum = dot(forward[:, :rows], pair)
        x_spec[2 * m] = spectrum[:, :lanes]
        x_spec[2 * m + 1] = spectrum[:, lanes:]
        first = jnp.concatenate([taps[2 * m + 1], taps[2 * m + 2 * core]], axis=1)
        second = jnp.concatenate([taps[2 * m + 2], taps[2 * m + 2 * core + 1]], axis=1)
        spectrum = dot(forward[...], jnp.concatenate([first, second], axis=0))
        h_spec[2 * m] = spectrum[:, :lanes]
        h_spec[2 * m + 1] = spectrum[:, lanes:]

    step = 8

    @pl.loop(0, rows // step)
    def _(t):
        re = pl.ds(pl.multiple_of(t * step, step), step)
        im = pl.ds(pl.multiple_of(rows + t * step, step), step)
        xr = [x_spec[j, re] for j in range(2 * blocks)]
        xi = [x_spec[j, im] for j in range(2 * blocks)]
        yr = [None] * blocks
        yi = [None] * blocks
        for lag in range(blocks):
            for side in range(2):
                hr = h_spec[2 * lag + side, re]
                hi = h_spec[2 * lag + side, im]
                for j in range(blocks - lag):
                    b = j + lag
                    ar, ai = xr[2 * j + side], xi[2 * j + side]
                    pr = ar * hr - ai * hi
                    pi = ar * hi + ai * hr
                    yr[b] = pr if yr[b] is None else yr[b] + pr
                    yi[b] = pi if yi[b] is None else yi[b] + pi
        for b in range(blocks):
            y_spec[b, re] = yr[b]
            y_spec[b, im] = yi[b]

    skip = skip_ref[...]

    @pl.loop(0, blocks // 2)
    def _(m):
        spectrum = jnp.concatenate([y_spec[2 * m], y_spec[2 * m + 1]], axis=1)
        convolved = dot(inverse[...], spectrum.astype(jnp.bfloat16))
        for s in range(2):
            b = 2 * m + s
            part = convolved[:, s * lanes : (s + 1) * lanes]
            direct = skip * own[b, 0].astype(jnp.float32)
            out_ref[b] = (own[b, 2].astype(jnp.float32) * (part + direct)).astype(jnp.bfloat16)


def convolve(core, own, other, skip, forward, inverse):
    blocks, _, rows, lanes = own.shape
    return pl.pallas_call(
        conv_kernel,
        in_specs=[SMEM] + [VMEM] * 5,
        out_specs=VMEM,
        out_shape=jax.ShapeDtypeStruct((blocks, rows, lanes), jnp.bfloat16),
        scratch_shapes=[
            pltpu.VMEM((2 * blocks + 2, rows, lanes), jnp.bfloat16),
            pltpu.VMEM((2 * blocks, 2 * rows, lanes), jnp.float32),
            pltpu.VMEM((2 * blocks, 2 * rows, lanes), jnp.float32),
            pltpu.VMEM((blocks, 2 * rows, lanes), jnp.float32),
        ],
        **room(20, 8 * 10**9, 8 * MIB),
    )(core, own, other, skip, forward, inverse)


def attend_kernel(core_ref, qk_own, k_other, v_own, v_other, out):
    blocks, rows, lanes = v_own.shape
    core = core_ref[0]
    row = lax.broadcasted_iota(jnp.int32, (rows, rows), 0)
    col = lax.broadcasted_iota(jnp.int32, (rows, rows), 1)
    on_diagonal = col <= row
    beside = jnp.full((rows, rows), core, jnp.int32) > 0
    ones = jnp.ones((rows, lanes), jnp.bfloat16)

    def scores(b, j):
        both = jnp.concatenate([qk_own[j, 1], k_other[j]], axis=0)
        s = lax.dot_general(
            qk_own[b, 0], both, (((1,), (1,)), ((), ())), preferred_element_type=jnp.float32
        )
        if j == b:
            own = jnp.where(on_diagonal, s[:, :rows], MASKED)
            other = jnp.where(beside, s[:, rows:], MASKED)
            s = jnp.concatenate([own, other], axis=1)
        return s

    order = list(range(blocks))[::-1]
    current = [scores(order[0], j) for j in range(order[0] + 1)]
    for i, b in enumerate(order):
        top = current[0]
        for s in current[1:]:
            top = jnp.maximum(top, s)
        top = jnp.max(top, axis=1, keepdims=True)
        later = order[i + 1] if i + 1 < blocks else -1
        following = []
        total = None
        for j in range(b + 1):
            if j <= later:
                following.append(scores(later, j))
            weights = jnp.exp2((current[j] - top) * TO_EXP2).astype(jnp.bfloat16)
            both = jnp.concatenate(
                [
                    jnp.concatenate([v_own[j], ones], axis=1),
                    jnp.concatenate([v_other[j], ones], axis=1),
                ],
                axis=0,
            )
            part = jnp.dot(weights, both, preferred_element_type=jnp.float32)
            total = part if total is None else total + part
        out[b, 0] = v_own[b]
        out[b, 1] = (total[:, :lanes] / total[:, lanes:]).astype(jnp.bfloat16)
        current = following


def attend(core, qk_own, k_other, v_own, v_other):
    blocks, rows, lanes = v_own.shape
    return pl.pallas_call(
        attend_kernel,
        in_specs=[SMEM] + [VMEM] * 4,
        out_specs=VMEM,
        out_shape=jax.ShapeDtypeStruct((blocks, 2, rows, lanes), jnp.bfloat16),
        **room(24, 8 * 10**9, 4 * MIB),
    )(core, qk_own, k_other, v_own, v_other)


def to_chips(array):
    flat = array.reshape(array.shape[0], -1, array.shape[-1])
    moved = lax.all_to_all(flat, "chip", split_axis=0, concat_axis=0, tiled=True)
    return moved.reshape(array.shape)


def swap(array):
    return lax.ppermute(array, "core", [(0, 1), (1, 0)])


def per_device(gate_input, value_input, filter_taps, skip_gain, queries, keys):
    chip = lax.axis_index("chip")
    core = lax.axis_index("core").astype(jnp.int32).reshape(1)
    own = to_chips(pack(value_input, filter_taps, gate_input))
    packed = pack_rest(queries, keys)
    own, packed = lax.optimization_barrier((own, packed))
    qk_own = to_chips(packed[0])
    skip = lax.dynamic_slice(skip_gain, (chip * HEAD_DIM,), (HEAD_DIM,)).reshape(1, HEAD_DIM)
    v_own = convolve(core, own, swap(own), skip, *packed[1:])
    qk_own, v_other = lax.optimization_barrier((qk_own, swap(v_own)))
    back = to_chips(attend(core, qk_own, swap(qk_own[:, 1]), v_own, v_other))
    mixed, attended = unpack(back)
    return (mixed, attended)


def solution(mesh):
    ctx, tp = mesh.devices.shape
    fine = Mesh(mesh.devices.reshape(ctx // CORES, CORES, tp), ("chip", "core", "tp"))
    rows = P(("chip", "core"), "tp")
    return jax.shard_map(
        per_device,
        mesh=fine,
        in_specs=(rows, rows, rows, P("tp"), rows, rows),
        out_specs=(rows, rows),
        check_vma=False,
    )
```

time: 104 us -> 79.4 us (0.76)
  starting transfers between devices: 32.8 us -> 12.7 us
  blocking collectives: 0 us -> 17.5 us
  local copies, waits for them, and re-layouts: 12.2 us -> 2.64 us
  Pallas kernels: 25.9 us -> 19.7 us
  waiting for transfers between devices: 30.9 us -> 25.6 us
    all_to_all x6 -> x2, starting transfers between devices: 27.7 us -> 9.65 us  [to_chips(): lax.all_to_all(flat, 'chip', split_axis=0, concat_axis=0, tiled=True)]
    all_to_all x0 -> x1, blocking collectives: none -> 17.5 us  [to_chips(): lax.all_to_all(flat, 'chip', split_axis=0, concat_axis=0, tiled=True)]
    all_to_all x6 -> x2, waiting for transfers between devices: 30.9 us -> 24.1 us  [to_chips(): lax.all_to_all(flat, 'chip', split_axis=0, concat_axis=0, tiled=True)]
    pallas_call x3 -> x5, Pallas kernels: 25.9 us -> 19.7 us  [the longest x1 9.15 us: convolve(): pl.pallas_call(conv_kernel, in_specs=[SMEM] + [VMEM] * 5, out_specs=VMEM,...]
    unnamed x21 -> x20, local copies, waits for them, and re-layouts: 8.07 us -> 2.53 us
    reshape x3 -> x0, local copies, waits for them, and re-layouts: 3 us -> none  [to_heads(): array.reshape(rows, channels // HEAD_DIM, HEAD_DIM).transpose(1, 0, 2)]
    ppermute x3, starting transfers between devices: 5.14 us -> 3.03 us  [swap(): return lax.ppermute(array, 'core', [(0, 1), (1, 0)])]
    ppermute x3, waiting for transfers between devices: 0.01 us -> 1.54 us  [swap(): return lax.ppermute(array, 'core', [(0, 1), (1, 0)])]
  transfers between devices with their start and end apart: 9 -> 5, of which waited for: 4 -> 3; matrix products, arithmetic and copies ran while one was open for 7% -> 0% of each run, Pallas kernels for 20% -> 12%
where the time goes in v1:
time: 79.4 us; the launch traced here: 78.8 us
  waiting for transfers between devices  25.6 us (32%)
  Pallas kernels  19.7 us (25%)
  blocking collectives  17.5 us (22%)
  starting transfers between devices  12.7 us (16%)
  local copies, waits for them, and re-layouts  2.64 us (3%)
    all_to_all x2, waiting for transfers between devices, to_chips(): lax.all_to_all(flat, 'chip', split_axis=0, concat_axis=0, tiled=True)  24.1 us
    all_to_all x1, blocking collectives, to_chips(): lax.all_to_all(flat, 'chip', split_axis=0, concat_axis=0, tiled=True)  17.5 us
    all_to_all x2, starting transfers between devices, to_chips(): lax.all_to_all(flat, 'chip', split_axis=0, concat_axis=0, tiled=True)  9.65 us
    pallas_call x1, Pallas kernels, convolve(): pl.pallas_call(conv_kernel, in_specs=[SMEM] + [VMEM] * 5, out_specs=VMEM,...  9.15 us
    pallas_call x1, Pallas kernels, attend(): pl.pallas_call(attend_kernel, in_specs=[SMEM] + [VMEM] * 4, out_specs=VME...  6.77 us
    ppermute x3, starting transfers between devices, swap(): return lax.ppermute(array, 'core', [(0, 1), (1, 0)])  3.03 us
    unnamed x20, local copies, waits for them, and re-layouts  2.53 us
    pallas_call x1, Pallas kernels, pack(): pl.pallas_call(functools.partial(pack_kernel, count=count, parts=parts),...  2.48 us
  transfers between devices with their start and end apart: 5, of which 3 were waited for; matrix products, arithmetic and copies ran while one was open for 0% of the time, Pallas kernels for 12%

profile of v1, /device:TPU:1, one launch (start us, length us, event | category | flops | bytes accessed | tf_op | source)
XLA Modules:
  0.0 78.8 jit_solution(13450352522590697988)
XLA Ops:
  0.6 0.0 copy-start
  0.6 2.5 %shard_map.95 = bf16[8,3,256,128]{3,2,1,0:T(8,128)(2,1)} custom-call(bf16[256,1024]{1,0:T(8,128)(2,1)} %refs_0_.1, f32[256,1024]{1,0:T(8,128)} %refs_1_.1, bf16[256,1024]{1,0:T(8,128)(2,1)} %refs_2_.1), custom_call_target="tpu_custom_call" | custom-call | bytes 6291456 | tf_op jit(solution)/shard_map/pallas_call | solution.py:89
  3.1 0.0 copy-start.2
  3.1 0.0 copy-start.3
  3.2 0.0 copy-start.4
  3.2 0.0 copy-start.5
  3.2 6.1 %all-to-all-start = ((bf16[8,768,128]{2,1,0:T(8,128)(2,1)}), bf16[8,768,128]{2,1,0:T(8,128)(2,1)S(1)}, u32[]{:S(2)}, u32[]{:S(2)}) async-start(bf16[8,768,128]{2,1,0:T(8,128)(2,1)} %bitcast.18), calls=%async_computation | async-start | bytes 3145728 | tf_op jit(solution)/shard_map/all_to_all | solution.py:293
  9.3 0.0 copy-done.2
  9.3 0.0 copy-done.3
  9.3 0.0 copy-done.4
  9.3 0.0 copy-done.5
  9.3 0.2 shard_map.96
  9.5 0.0 copy-start.1
  9.6 1.0 %copy-done.1 = bf16[8,2,256,128]{3,2,1,0:T(8,128)(2,1)} copy-done((bf16[8,2,256,128]{3,2,1,0:T(8,128)(2,1)}, bf16[8,2,256,128]{3,2,1,0:T(8,128)(2,1)S(1)}, u32[]{:S(2)}) %copy-start.1) | copy-done | bytes 1048600
  10.5 0.0 copy-start.6
  10.6 0.8 %copy-done.6 = bf16[512,512]{1,0:T(8,128)(2,1)} copy-done((bf16[512,512]{1,0:T(8,128)(2,1)}, bf16[512,512]{1,0:T(8,128)(2,1)S(1)}, u32[]{:S(2)}) %copy-start.6) | copy-done | bytes 524312
  11.3 0.0 copy-start.8
  11.3 0.7 copy-done.8
  12.0 17.7 %all-to-all-done = bf16[8,768,128]{2,1,0:T(8,128)(2,1)S(1)} async-done(((bf16[8,768,128]{2,1,0:T(8,128)(2,1)}), bf16[8,768,128]{2,1,0:T(8,128)(2,1)S(1)}, u32[]{:S(2)}, u32[]{:S(2)}) %all-to-all-start) | async-done | bytes 1572896 | tf_op jit(solution)/shard_map/all_to_all | solution.py:293
  29.7 0.0 copy-start.7
  29.7 0.0 copy-start.9
  29.7 1.9 %collective-permute-start = (bf16[8,3,256,128]{3,2,1,0:T(8,128)(2,1)S(1)}, bf16[8,3,256,128]{3,2,1,0:T(8,128)(2,1)}, u32[]{:S(2)}, u32[]{:S(2)}) collective-permute-start(bf16[8,3,256,128]{3,2,1,0:T(8,128)(2,1)S(1)} %bitcast.14), channel_id=1, source_target_pairs={{0,8},{8,0},{1,9},{9,1},{2,10},{10,2},{3,11},{11,3},{4,12},{12,4},... | collective-permute-start | bytes 4718600 | tf_op jit(solution)/shard_map/ppermute | solution.py:298
  31.6 0.0 copy-done
  31.6 0.1 dynamic-slice_bitcast_fusion.skip_ref
  31.7 3.6 %all-to-all-start.1 = ((bf16[8,512,128]{2,1,0:T(8,128)(2,1)}), bf16[8,512,128]{2,1,0:T(8,128)(2,1)S(1)}, u32[]{:S(2)}, u32[]{:S(2)}) async-start(bf16[8,512,128]{2,1,0:T(8,128)(2,1)} %bitcast.16), calls=%async_computation.1 | async-start | bytes 2097152 | tf_op jit(solution)/shard_map/all_to_all | solution.py:293
  35.2 0.0 collective-permute-done.other
  35.2 0.0 copy-done.7
  35.3 0.0 copy-done.9
  35.3 9.1 %shard_map.97.v_own = bf16[8,256,128]{2,1,0:T(8,128)(2,1)} custom-call(s32[1]{0:T(128)} %bitcast.core_ref, bf16[8,3,256,128]{3,2,1,0:T(8,128)(2,1)S(1)} %bitcast.15, bf16[8,3,256,128]{3,2,1,0:T(8,128)(2,1)} %collective-permute-done.other, f32[1,128]{1,0:T(1,128)S(1)} %dynamic-slice_bitcast_fusion.skip_ref, bf16[512,512]{1,0:T(8,128)(2,1)S(1)} %copy-done.7, ...), custom_call_target="tpu_custom_call" | custom-call | flops 8000000000 | bytes 8388608 | tf_op jit(solution)/shard_map/pallas_call | solution.py:217
  44.4 0.1 collective-permute-start.1
  44.5 6.4 %all-to-all-done.1 = bf16[8,512,128]{2,1,0:T(8,128)(2,1)S(1)} async-done(((bf16[8,512,128]{2,1,0:T(8,128)(2,1)}), bf16[8,512,128]{2,1,0:T(8,128)(2,1)S(1)}, u32[]{:S(2)}, u32[]{:S(2)}) %all-to-all-start.1) | async-done | bytes 1048608 | tf_op jit(solution)/shard_map/all_to_all | solution.py:293
  50.9 0.0 collective-permute-done.1.v_other
  51.0 1.0 %collective-permute-start.2 = (bf16[8,256,128]{2,1,0:T(8,128)(2,1)S(1)}, bf16[8,256,128]{2,1,0:T(8,128)(2,1)S(1)}, u32[]{:S(2)}, u32[]{:S(2)}) collective-permute-start(bf16[8,256,128]{2,1,0:T(8,128)(2,1)S(1)} %slice_bitcast_fusion), channel_id=1, source_target_pairs={{0,8},{8,0},{1,9},{9,1},{2,10},{10,2},{3,11},{11,3},{4,12},{12,4},... | collective-permute-start | bytes 1572872 | tf_op jit(solution)/shard_map/ppermute | solution.py:298
  52.0 1.5 %collective-permute-done.2.k_other = bf16[8,256,128]{2,1,0:T(8,128)(2,1)S(1)} collective-permute-done((bf16[8,256,128]{2,1,0:T(8,128)(2,1)S(1)}, bf16[8,256,128]{2,1,0:T(8,128)(2,1)S(1)}, u32[]{:S(2)}, u32[]{:S(2)}) %collective-permute-start.2) | collective-permute-done | bytes 524320 | tf_op jit(solution)/shard_map/ppermute | solution.py:298
  53.5 6.8 %shard_map.98 = bf16[8,2,256,128]{3,2,1,0:T(8,128)(2,1)S(1)} custom-call(s32[1]{0:T(128)} %bitcast.core_ref, bf16[8,2,256,128]{3,2,1,0:T(8,128)(2,1)S(1)} %bitcast.13, bf16[8,256,128]{2,1,0:T(8,128)(2,1)S(1)} %collective-permute-done.2.k_other, bf16[8,256,128]{2,1,0:T(8,128)(2,1)} %shard_map.97.v_own, bf16[8,256,128]{2,1,0:T(8,128)(2,1)S(1)} %collective-permute-done.1.v_other), custom_call_target="tpu_custom_call" | custom-call | flops 8000000000 | bytes 4194304 | tf_op jit(solution)/shard_map/pallas_call | solution.py:282
  60.3 17.5 %all_to_all.15 = bf16[8,512,128]{2,1,0:T(8,128)(2,1)S(1)} all-to-all(bf16[8,512,128]{2,1,0:T(8,128)(2,1)S(1)} %bitcast.17), channel_id=1, replica_groups=mesh['chip'=8,'core'=2,'tp'=8] {'chip'}, dimensions={0} | all-to-all | bytes 2097152 | tf_op jit(solution)/shard_map/all_to_all | solution.py:293
  77.8 1.1 %shard_map.99 = (bf16[256,1024]{1,0:T(8,128)(2,1)}, bf16[256,1024]{1,0:T(8,128)(2,1)}) custom-call(bf16[8,2,256,128]{3,2,1,0:T(8,128)(2,1)S(1)} %bitcast.11), custom_call_target="tpu_custom_call" | custom-call | bytes 2097152 | tf_op jit(solution)/shard_map/pallas_call | solution.py:139
  (1 shorter events, 0.0 us)
Async XLA Ops:
  0.6 31.0 %copy-start = (f32[1024]{0:T(1024)S(1)}, f32[1024]{0:T(1024)}, u32[]{:S(2)}) copy-start(f32[1024]{0:T(1024)} %param.11) | copy-start | bytes 12292
  3.1 6.1 %copy-start.2 = (bf16[256,1024]{1,0:T(8,128)(2,1)S(1)}, bf16[256,1024]{1,0:T(8,128)(2,1)}, u32[]{:S(2)}) copy-start(bf16[256,1024]{1,0:T(8,128)(2,1)} %queries.1) | copy-start | bytes 1572868
  3.1 6.1 %copy-start.3 = (bf16[256,1024]{1,0:T(8,128)(2,1)S(1)}, bf16[256,1024]{1,0:T(8,128)(2,1)}, u32[]{:S(2)}) copy-start(bf16[256,1024]{1,0:T(8,128)(2,1)} %keys.1) | copy-start | bytes 1572868
  3.2 6.1 %copy-start.4 = (bf16[512,512]{1,0:T(8,128)(2,1)S(1)}, bf16[512,512]{1,0:T(8,128)(2,1)}, u32[]{:S(2)}) copy-start(bf16[512,512]{1,0:T(8,128)(2,1)} %constant.21.clone.forward) | copy-start | bytes 1572868
  3.2 6.1 %copy-start.5 = (bf16[256,512]{1,0:T(8,128)(2,1)S(1)}, bf16[256,512]{1,0:T(8,128)(2,1)}, u32[]{:S(2)}) copy-start(bf16[256,512]{1,0:T(8,128)(2,1)} %constant.22.clone.inverse) | copy-start | bytes 786436
  3.2 26.5 %all-to-all-start = ((bf16[8,768,128]{2,1,0:T(8,128)(2,1)}), bf16[8,768,128]{2,1,0:T(8,128)(2,1)S(1)}, u32[]{:S(2)}, u32[]{:S(2)}) async-start(bf16[8,768,128]{2,1,0:T(8,128)(2,1)} %bitcast.18), calls=%async_computation | async-start | bytes 3145728 | tf_op jit(solution)/shard_map/all_to_all | solution.py:293
  9.5 1.0 %copy-start.1 = (bf16[8,2,256,128]{3,2,1,0:T(8,128)(2,1)}, bf16[8,2,256,128]{3,2,1,0:T(8,128)(2,1)S(1)}, u32[]{:S(2)}) copy-start(bf16[8,2,256,128]{3,2,1,0:T(8,128)(2,1)S(1)} %get-tuple-element.14) | copy-start | bytes 3145732
  10.5 0.8 %copy-start.6 = (bf16[512,512]{1,0:T(8,128)(2,1)}, bf16[512,512]{1,0:T(8,128)(2,1)S(1)}, u32[]{:S(2)}) copy-start(bf16[512,512]{1,0:T(8,128)(2,1)S(1)} %get-tuple-element.16.forward) | copy-start | bytes 1572868
  11.3 0.7 copy-start.8
  29.7 5.5 %copy-start.7 = (bf16[512,512]{1,0:T(8,128)(2,1)S(1)}, bf16[512,512]{1,0:T(8,128)(2,1)}, u32[]{:S(2)}) copy-start(bf16[512,512]{1,0:T(8,128)(2,1)} %copy-done.6) | copy-start | bytes 1572868
  29.7 5.5 %copy-start.9 = (bf16[256,512]{1,0:T(8,128)(2,1)S(1)}, bf16[256,512]{1,0:T(8,128)(2,1)}, u32[]{:S(2)}) copy-start(bf16[256,512]{1,0:T(8,128)(2,1)} %copy-done.8) | copy-start | bytes 786436
  29.7 5.5 %collective-permute-start = (bf16[8,3,256,128]{3,2,1,0:T(8,128)(2,1)S(1)}, bf16[8,3,256,128]{3,2,1,0:T(8,128)(2,1)}, u32[]{:S(2)}, u32[]{:S(2)}) collective-permute-start(bf16[8,3,256,128]{3,2,1,0:T(8,128)(2,1)S(1)} %bitcast.14), channel_id=1, source_target_pairs={{0,8},{8,0},{1,9},{9,1},{2,10},{10,2},{3,11},{11,3},{4,12},{12,4},... | collective-permute-start | bytes 4718600 | tf_op jit(solution)/shard_map/ppermute | solution.py:298
  31.7 19.2 %all-to-all-start.1 = ((bf16[8,512,128]{2,1,0:T(8,128)(2,1)}), bf16[8,512,128]{2,1,0:T(8,128)(2,1)S(1)}, u32[]{:S(2)}, u32[]{:S(2)}) async-start(bf16[8,512,128]{2,1,0:T(8,128)(2,1)} %bitcast.16), calls=%async_computation.1 | async-start | bytes 2097152 | tf_op jit(solution)/shard_map/all_to_all | solution.py:293
  44.4 6.5 %collective-permute-start.1 = (bf16[8,256,128]{2,1,0:T(8,128)(2,1)}, bf16[8,256,128]{2,1,0:T(8,128)(2,1)S(1)}, u32[]{:S(2)}, u32[]{:S(2)}) collective-permute-start(bf16[8,256,128]{2,1,0:T(8,128)(2,1)} %shard_map.97.v_own), channel_id=1, source_target_pairs={{0,8},{8,0},{1,9},{9,1},{2,10},{10,2},{3,11},{11,3},{4,12},{12,4},... | collective-permute-start | bytes 1572872 | tf_op jit(solution)/shard_map/ppermute | solution.py:298
  51.0 2.6 %collective-permute-start.2 = (bf16[8,256,128]{2,1,0:T(8,128)(2,1)S(1)}, bf16[8,256,128]{2,1,0:T(8,128)(2,1)S(1)}, u32[]{:S(2)}, u32[]{:S(2)}) collective-permute-start(bf16[8,256,128]{2,1,0:T(8,128)(2,1)S(1)} %slice_bitcast_fusion), channel_id=1, source_target_pairs={{0,8},{8,0},{1,9},{9,1},{2,10},{10,2},{3,11},{11,3},{4,12},{12,4},... | collective-permute-start | bytes 1572872 | tf_op jit(solution)/shard_map/ppermute | solution.py:298

commit v2 on v1

--- a/solution.py
+++ b/solution.py
@@ -14,6 +14,7 @@
 CORES = 2
 SCALE = 1.0 / math.sqrt(HEAD_DIM)
 MASKED = -1e30
+PARTS = 2
 TO_EXP2 = SCALE * math.log2(math.e)
 MIB = 1024 * 1024
 
@@ -23,7 +24,8 @@
     freq = np.arange(rows, dtype=np.float64)[:, None] + 0.5
     time = np.arange(period, dtype=np.float64)[None, :]
     angle = 2.0 * np.pi * freq * time / period
-    forward = np.concatenate([np.cos(angle), -np.sin(angle)], axis=0)
+    first = angle[:, :rows]
+    forward = np.concatenate([np.cos(first), -np.sin(first)], axis=0)
     later = angle[:, rows:].T
     inverse = np.concatenate([np.cos(later), -np.sin(later)], axis=1) / rows
     return jnp.asarray(forward, jnp.bfloat16), jnp.asarray(inverse, jnp.bfloat16)
@@ -94,31 +96,31 @@
         scratch_shapes=[pltpu.VMEM(a.shape, a.dtype) for a in arrays]
         + [pltpu.VMEM(shape, jnp.bfloat16)]
         + [pltpu.SemaphoreType.DMA((count, parts))] * 2,
-        **room(56, 0, 6 * MIB),
-    )(*arrays)
-
-
-def pack_rest_kernel(queries, keys, forward, inverse, out, forward_out, inverse_out):
+        **room(24, 0, 6 * MIB),
+    )(*[in_hbm(a) for a in arrays])
+
+
+def pack_rest_kernel(queries, keys, forward, out, forward_out):
     for p in range(out.shape[0]):
         lanes = slice(p * HEAD_DIM, (p + 1) * HEAD_DIM)
         out[p, 0] = queries[:, lanes]
         out[p, 1] = keys[:, lanes]
     forward_out[...] = forward[...]
-    inverse_out[...] = inverse[...]
-
-
-def pack_rest(queries, keys):
+
+
+def pack_rest(queries, keys, forward):
     rows, channels = queries.shape
-    chips = channels // HEAD_DIM
-    tables = transform_tables(rows)
-    out = jax.ShapeDtypeStruct((chips, 2, rows, HEAD_DIM), jnp.bfloat16)
+    shape = (channels // HEAD_DIM, 2, rows, HEAD_DIM)
     return pl.pallas_call(
         pack_rest_kernel,
-        in_specs=[VMEM] * 4,
-        out_specs=[VMEM] * 3,
-        out_shape=[out] + [jax.ShapeDtypeStruct(t.shape, t.dtype) for t in tables],
-        **room(16, 0, 6 * MIB),
-    )(queries, keys, *tables)
+        in_specs=[VMEM] * 3,
+        out_specs=[VMEM] * 2,
+        out_shape=[
+            jax.ShapeDtypeStruct(shape, jnp.bfloat16),
+            jax.ShapeDtypeStruct(forward.shape, jnp.bfloat16),
+        ],
+        **room(16, 0, 2 * MIB),
+    )(queries, keys, forward)
 
 
 def unpack_kernel(back, mixed, attended, sems):
@@ -146,35 +148,40 @@
     )(back)
 
 
-def conv_kernel(core_ref, own, other, skip_ref, forward, inverse, out_ref, taps, *specs):
-    x_spec, h_spec, y_spec = specs
+def conv_kernel(core_ref, own, x_other, h_any, skip_ref, forward, inverse_any, *refs):
+    outs, refs = refs[:PARTS], refs[PARTS:]
+    x_spec, h_spec, y_spec, made, h_other, inverse, tap_sem, table_sem, out_sem = refs
     blocks, _, rows, lanes = own.shape
     core = core_ref[0]
+    copy = pltpu.make_async_copy
+    half = blocks // PARTS
+    taps = [
+        copy(h_any.at[pl.ds(s * half, half)], h_other.at[pl.ds(s * half, half)], tap_sem.at[s])
+        for s in range(PARTS)
+    ]
+    table = copy(inverse_any, inverse, table_sem.at[0])
+    for c in taps + [table]:
+        c.start()
 
     def dot(a, b):
         return jnp.dot(a, b, preferred_element_type=jnp.float32)
 
-    taps[0] = jnp.zeros((rows, lanes), jnp.bfloat16)
-    taps[1] = jnp.zeros((rows, lanes), jnp.bfloat16)
-
-    @pl.loop(0, blocks)
-    def _(m):
-        taps[2 * m + 2 + core] = own[m, 1]
-        taps[2 * m + 3 - core] = other[m, 1]
-
-    @pl.loop(0, blocks)
-    def _(m):
-        pair = jnp.concatenate([own[m, 0], other[m, 0]], axis=1)
-        spectrum = dot(forward[:, :rows], pair)
-        x_spec[2 * m] = spectrum[:, :lanes]
-        x_spec[2 * m + 1] = spectrum[:, lanes:]
-        first = jnp.concatenate([taps[2 * m + 1], taps[2 * m + 2 * core]], axis=1)
-        second = jnp.concatenate([taps[2 * m + 2], taps[2 * m + 2 * core + 1]], axis=1)
-        spectrum = dot(forward[...], jnp.concatenate([first, second], axis=0))
-        h_spec[2 * m] = spectrum[:, :lanes]
-        h_spec[2 * m + 1] = spectrum[:, lanes:]
+    h_spec[0] = jnp.zeros((2 * rows, lanes), jnp.float32)
+    h_spec[1] = jnp.zeros((2 * rows, lanes), jnp.float32)
+    for side in range(2):
+        for m in range(blocks):
+            if side == 1 and m % half == 0:
+                taps[m // half].wait()
+            pair = (x_other[m], h_other[m]) if side else (own[m, 0], own[m, 1])
+            both = jnp.concatenate(pair, axis=1)
+            spectrum = dot(forward[...], both)
+            x_spec[2 * m + side] = spectrum[:, :lanes]
+            at = 2 * m + 2 + (core if side == 0 else 1 - core)
+            h_spec[at] = spectrum[:, lanes:]
 
     step = 8
+    row = lax.broadcasted_iota(jnp.int32, (step, lanes), 0)
+    sign = 1.0 - 2.0 * (row % 2).astype(jnp.float32)
 
     @pl.loop(0, rows // step)
     def _(t):
@@ -186,8 +193,9 @@
         yi = [None] * blocks
         for lag in range(blocks):
             for side in range(2):
-                hr = h_spec[2 * lag + side, re]
-                hi = h_spec[2 * lag + side, im]
+                k = 2 * lag + 1 if side == 0 else 2 * lag + 2 * core
+                hr = h_spec[k, re] + sign * h_spec[k + 1, im]
+                hi = h_spec[k, im] - sign * h_spec[k + 1, re]
                 for j in range(blocks - lag):
                     b = j + lag
                     ar, ai = xr[2 * j + side], xi[2 * j + side]
@@ -196,41 +204,63 @@
                     yr[b] = pr if yr[b] is None else yr[b] + pr
                     yi[b] = pi if yi[b] is None else yi[b] + pi
         for b in range(blocks):
-            y_spec[b, re] = yr[b]
-            y_spec[b, im] = yi[b]
-
+            y_spec[re, b * lanes : (b + 1) * lanes] = yr[b]
+            y_spec[im, b * lanes : (b + 1) * lanes] = yi[b]
+
+    table.wait()
     skip = skip_ref[...]
-
-    @pl.loop(0, blocks // 2)
-    def _(m):
-        spectrum = jnp.concatenate([y_spec[2 * m], y_spec[2 * m + 1]], axis=1)
+    stores = []
+    for m in range(blocks // 2):
+        spectrum = y_spec[:, 2 * m * lanes : 2 * (m + 1) * lanes]
         convolved = dot(inverse[...], spectrum.astype(jnp.bfloat16))
         for s in range(2):
             b = 2 * m + s
             part = convolved[:, s * lanes : (s + 1) * lanes]
             direct = skip * own[b, 0].astype(jnp.float32)
-            out_ref[b] = (own[b, 2].astype(jnp.float32) * (part + direct)).astype(jnp.bfloat16)
-
-
-def convolve(core, own, other, skip, forward, inverse):
+            made[b] = (own[b, 2].astype(jnp.float32) * (part + direct)).astype(jnp.bfloat16)
+            stores.append(copy(made.at[b], outs[b // half].at[b % half], out_sem.at[b]))
+            stores[-1].start()
+    for c in stores:
+        c.wait()
+
+
+def in_hbm(array):
+    return pltpu.with_memory_space_constraint(array, pltpu.HBM)
+
+
+def convolve(core, own, x_other, h_other, skip, forward, inverse):
     blocks, _, rows, lanes = own.shape
     return pl.pallas_call(
         conv_kernel,
-        in_specs=[SMEM] + [VMEM] * 5,
-        out_specs=VMEM,
-        out_shape=jax.ShapeDtypeStruct((blocks, rows, lanes), jnp.bfloat16),
+        in_specs=[SMEM, VMEM, VMEM, ANYWHERE, VMEM, VMEM, ANYWHERE],
+        out_specs=[pl.BlockSpec(memory_space=pltpu.HBM)] * PARTS,
+        out_shape=[jax.ShapeDtypeStruct((blocks // PARTS, rows, lanes), jnp.bfloat16)] * PARTS,
         scratch_shapes=[
-            pltpu.VMEM((2 * blocks + 2, rows, lanes), jnp.bfloat16),
             pltpu.VMEM((2 * blocks, 2 * rows, lanes), jnp.float32),
-            pltpu.VMEM((2 * blocks, 2 * rows, lanes), jnp.float32),
-            pltpu.VMEM((blocks, 2 * rows, lanes), jnp.float32),
+            pltpu.VMEM((2 * blocks + 2, 2 * rows, lanes), jnp.float32),
+            pltpu.VMEM((2 * rows, blocks * lanes), jnp.float32),
+            pltpu.VMEM((blocks, rows, lanes), jnp.bfloat16),
+            pltpu.VMEM((blocks, rows, lanes), jnp.bfloat16),
+            pltpu.VMEM(inverse.shape, jnp.bfloat16),
+            pltpu.SemaphoreType.DMA((PARTS,)),
+            pltpu.SemaphoreType.DMA((1,)),
+            pltpu.SemaphoreType.DMA((blocks,)),
         ],
-        **room(20, 8 * 10**9, 8 * MIB),
-    )(core, own, other, skip, forward, inverse)
-
-
-def attend_kernel(core_ref, qk_own, k_other, v_own, v_other, out):
-    blocks, rows, lanes = v_own.shape
+        **room(24, 10**6, MIB),
+    )(core, own, x_other, in_hbm(h_other), skip, forward, in_hbm(inverse))
+
+
+def attend_kernel(core_ref, qk_own, k_other, *refs):
+    v_any, v_other, refs = refs[:PARTS], refs[PARTS : 2 * PARTS], refs[2 * PARTS :]
+    out, v_own, v_sem = refs
+    blocks, _, rows, lanes = qk_own.shape
+    each = blocks // PARTS
+    values = [
+        pltpu.make_async_copy(part, v_own.at[pl.ds(i * each, each)], v_sem.at[i])
+        for i, part in enumerate(v_any)
+    ]
+    for c in values:
+        c.start()
     core = core_ref[0]
     row = lax.broadcasted_iota(jnp.int32, (rows, rows), 0)
     col = lax.broadcasted_iota(jnp.int32, (rows, rows), 1)
@@ -238,19 +268,27 @@
     beside = jnp.full((rows, rows), core, jnp.int32) > 0
     ones = jnp.ones((rows, lanes), jnp.bfloat16)
 
-    def scores(b, j):
-        both = jnp.concatenate([qk_own[j, 1], k_other[j]], axis=0)
-        s = lax.dot_general(
-            qk_own[b, 0], both, (((1,), (1,)), ((), ())), preferred_element_type=jnp.float32
+    def product(q, k):
+        return lax.dot_general(
+            q, k, (((1,), (1,)), ((), ())), preferred_element_type=jnp.float32
         )
+
+    def masked(b, j, s):
         if j == b:
             own = jnp.where(on_diagonal, s[:, :rows], MASKED)
             other = jnp.where(beside, s[:, rows:], MASKED)
             s = jnp.concatenate([own, other], axis=1)
         return s
 
+    def scores(b, j):
+        both = jnp.concatenate([qk_own[j, 1], k_other[j]], axis=0)
+        return masked(b, j, product(qk_own[b, 0], both))
+
     order = list(range(blocks))[::-1]
-    current = [scores(order[0], j) for j in range(order[0] + 1)]
+    last = order[0]
+    current = [scores(last, j) for j in range(blocks)]
+    for c in values:
+        c.wait()
     for i, b in enumerate(order):
         top = current[0]
         for s in current[1:]:
@@ -266,7 +304,7 @@
             both = jnp.concatenate(
                 [
                     jnp.concatenate([v_own[j], ones], axis=1),
-                    jnp.concatenate([v_other[j], ones], axis=1),
+                    jnp.concatenate([v_other[j // each][j % each], ones], axis=1),
                 ],
                 axis=0,
             )
@@ -278,14 +316,18 @@
 
 
 def attend(core, qk_own, k_other, v_own, v_other):
-    blocks, rows, lanes = v_own.shape
+    blocks, _, rows, lanes = qk_own.shape
     return pl.pallas_call(
         attend_kernel,
-        in_specs=[SMEM] + [VMEM] * 4,
+        in_specs=[SMEM] + [VMEM] * 2 + [ANYWHERE] * PARTS + [VMEM] * PARTS,
         out_specs=VMEM,
         out_shape=jax.ShapeDtypeStruct((blocks, 2, rows, lanes), jnp.bfloat16),
-        **room(24, 8 * 10**9, 4 * MIB),
-    )(core, qk_own, k_other, v_own, v_other)
+        scratch_shapes=[
+            pltpu.VMEM((blocks, rows, lanes), jnp.bfloat16),
+            pltpu.SemaphoreType.DMA((PARTS,)),
+        ],
+        **room(24, 10**9, MIB),
+    )(core, qk_own, k_other, *[in_hbm(v) for v in v_own], *v_other)
 
 
 def to_chips(array):
@@ -302,13 +344,16 @@
     chip = lax.axis_index("chip")
     core = lax.axis_index("core").astype(jnp.int32).reshape(1)
     own = to_chips(pack(value_input, filter_taps, gate_input))
-    packed = pack_rest(queries, keys)
+    forward, inverse = transform_tables(queries.shape[0])
+    packed = pack_rest(queries, keys, forward)
     own, packed = lax.optimization_barrier((own, packed))
     qk_own = to_chips(packed[0])
+    x_other, h_other = (swap(own[:, i]) for i in (0, 1))
     skip = lax.dynamic_slice(skip_gain, (chip * HEAD_DIM,), (HEAD_DIM,)).reshape(1, HEAD_DIM)
-    v_own = convolve(core, own, swap(own), skip, *packed[1:])
-    qk_own, v_other = lax.optimization_barrier((qk_own, swap(v_own)))
-    back = to_chips(attend(core, qk_own, swap(qk_own[:, 1]), v_own, v_other))
+    v_own = convolve(core, own, x_other, h_other, skip, packed[1], inverse)
+    qk_own, v_other = lax.optimization_barrier((qk_own, [swap(v) for v in v_own]))
+    k_other = swap(qk_own[:, 1])
+    back = to_chips(attend(core, qk_own, k_other, v_own, v_other))
     mixed, attended = unpack(back)
     return (mixed, attended)
 

time: 79.4 us -> 78.1 us (0.984)
  waiting for transfers between devices: 25.6 us -> 22.6 us
  Pallas kernels: 19.7 us -> 17.2 us
  starting transfers between devices: 12.7 us -> 14.5 us
  local copies, waits for them, and re-layouts: 2.64 us -> 4.15 us
    all_to_all x2, waiting for transfers between devices: 24.1 us -> 17.3 us  [to_chips(): lax.all_to_all(flat, 'chip', split_axis=0, concat_axis=0, tiled=True)]
    ppermute x3 -> x5, waiting for transfers between devices: 1.54 us -> 5.35 us  [swap(): return lax.ppermute(array, 'core', [(0, 1), (1, 0)])]
    pallas_call x3, Pallas kernels: 16.1 us -> 13.6 us  [the longest x1 7.13 us: convolve(): pl.pallas_call(conv_kernel, in_specs=[SMEM, VMEM, VMEM, ANYWHERE, VMEM, V...]
    ppermute x3 -> x5, starting transfers between devices: 3.03 us -> 4.63 us  [swap(): return lax.ppermute(array, 'core', [(0, 1), (1, 0)])]
    squeeze x1 -> x2, local copies, waits for them, and re-layouts: 0.03 us -> 1.07 us  [the longest x1 1.04 us: per_device(): x_other, h_other = (swap(own[:, i]) for i in (0, 1))]
    unnamed x20 -> x14, local copies, waits for them, and re-layouts: 2.53 us -> 3 us
  transfers between devices with their start and end apart: 5 -> 7, of which waited for: 3 -> 6; matrix products, arithmetic and copies ran while one was open for 0% -> 1% of each run, Pallas kernels for 12% -> 9%
where the time goes in v2:
time: 78.1 us; the launch traced here: 77.2 us
  waiting for transfers between devices  22.6 us (29%)
  blocking collectives  18 us (23%)
  Pallas kernels  17.2 us (22%)
  starting transfers between devices  14.5 us (19%)
  local copies, waits for them, and re-layouts  4.15 us (5%)
    all_to_all x1, blocking collectives, to_chips(): lax.all_to_all(flat, 'chip', split_axis=0, concat_axis=0, tiled=True)  18 us
    all_to_all x2, waiting for transfers between devices, to_chips(): lax.all_to_all(flat, 'chip', split_axis=0, concat_axis=0, tiled=True)  17.3 us
    all_to_all x2, starting transfers between devices, to_chips(): lax.all_to_all(flat, 'chip', split_axis=0, concat_axis=0, tiled=True)  9.87 us
    pallas_call x1, Pallas kernels, convolve(): pl.pallas_call(conv_kernel, in_specs=[SMEM, VMEM, VMEM, ANYWHERE, VMEM, V...  7.13 us
    pallas_call x1, Pallas kernels, attend(): pl.pallas_call(attend_kernel, in_specs=[SMEM] + [VMEM] * 2 + [ANYWHERE] *...  6.3 us
    ppermute x5, waiting for transfers between devices, swap(): return lax.ppermute(array, 'core', [(0, 1), (1, 0)])  5.35 us
    ppermute x5, starting transfers between devices, swap(): return lax.ppermute(array, 'core', [(0, 1), (1, 0)])  4.63 us
    unnamed x14, local copies, waits for them, and re-layouts  3 us
  transfers between devices with their start and end apart: 7, of which 6 were waited for; matrix products, arithmetic and copies ran while one was open for 1% of the time, Pallas kernels for 9%

profile of v2, /device:TPU:1, one launch (start us, length us, event | category | flops | bytes accessed | tf_op | source)
XLA Modules:
  0.0 77.2 jit_solution(4670705847098921270)
XLA Ops:
  0.6 0.0 copy-start
  0.6 2.5 %shard_map.95 = bf16[8,3,256,128]{3,2,1,0:T(8,128)(2,1)} custom-call(bf16[256,1024]{1,0:T(8,128)(2,1)} %refs_0_.1, f32[256,1024]{1,0:T(8,128)} %refs_1_.1, bf16[256,1024]{1,0:T(8,128)(2,1)} %refs_2_.1), custom_call_target="tpu_custom_call" | custom-call | bytes 6291456 | tf_op jit(solution)/shard_map/pallas_call | solution.py:91
  3.2 0.0 copy-start.2
  3.2 6.1 %all-to-all-start = ((bf16[8,768,128]{2,1,0:T(8,128)(2,1)}), bf16[8,768,128]{2,1,0:T(8,128)(2,1)S(1)}, u32[]{:S(2)}, u32[]{:S(2)}) async-start(bf16[8,768,128]{2,1,0:T(8,128)(2,1)} %bitcast.1), calls=%async_computation | async-start | bytes 3145728 | tf_op jit(solution)/shard_map/all_to_all | solution.py:335
  9.3 0.0 copy-done.2
  9.3 0.0 copy-start.3
  9.3 1.0 %copy-done.3 = bf16[256,1024]{1,0:T(8,128)(2,1)S(1)} copy-done((bf16[256,1024]{1,0:T(8,128)(2,1)S(1)}, bf16[256,1024]{1,0:T(8,128)(2,1)}, u32[]{:S(2)}) %copy-start.3) | copy-done | bytes 524312
  10.3 0.0 copy-start.4
  10.3 0.9 %copy-done.4 = bf16[512,256]{1,0:T(8,128)(2,1)S(1)} copy-done((bf16[512,256]{1,0:T(8,128)(2,1)S(1)}, bf16[512,256]{1,0:T(8,128)(2,1)}, u32[]{:S(2)}) %copy-start.4) | copy-done | bytes 262168
  11.3 0.2 shard_map.96
  11.5 0.0 copy-start.1
  11.5 1.0 %copy-done.1 = bf16[8,2,256,128]{3,2,1,0:T(8,128)(2,1)} copy-done((bf16[8,2,256,128]{3,2,1,0:T(8,128)(2,1)}, bf16[8,2,256,128]{3,2,1,0:T(8,128)(2,1)S(1)}, u32[]{:S(2)}) %copy-start.1) | copy-done | bytes 1048600
  12.5 17.3 %all-to-all-done = bf16[8,768,128]{2,1,0:T(8,128)(2,1)S(1)} async-done(((bf16[8,768,128]{2,1,0:T(8,128)(2,1)}), bf16[8,768,128]{2,1,0:T(8,128)(2,1)S(1)}, u32[]{:S(2)}, u32[]{:S(2)}) %all-to-all-start) | async-done | bytes 1572896 | tf_op jit(solution)/shard_map/all_to_all | solution.py:335
  29.7 3.8 %all-to-all-start.1 = ((bf16[8,512,128]{2,1,0:T(8,128)(2,1)}), bf16[8,512,128]{2,1,0:T(8,128)(2,1)S(1)}, u32[]{:S(2)}, u32[]{:S(2)}) async-start(bf16[8,512,128]{2,1,0:T(8,128)(2,1)} %bitcast.20), calls=%async_computation.1 | async-start | bytes 2097152 | tf_op jit(solution)/shard_map/all_to_all | solution.py:335
  33.5 1.0 %slice_bitcast_fusion.1 = (bf16[8,256,128]{2,1,0:T(8,128)(2,1)}, bf16[8,256,128]{2,1,0:T(8,128)(2,1)}) fusion(bf16[8,3,256,128]{3,2,1,0:T(8,128)(2,1)S(1)} %bitcast.15), kind=kLoop, calls=%fused_computation.1 | loop fusion | bytes 2097152 | tf_op jit(solution)/shard_map/squeeze | solution.py:351
  34.5 1.6 %collective-permute-start.1 = (bf16[8,256,128]{2,1,0:T(8,128)(2,1)}, bf16[8,256,128]{2,1,0:T(8,128)(2,1)}, u32[]{:S(2)}, u32[]{:S(2)}) collective-permute-start(bf16[8,256,128]{2,1,0:T(8,128)(2,1)} %get-tuple-element.22), channel_id=1, source_target_pairs={{0,8},{8,0},{1,9},{9,1},{2,10},{10,2},{3,11},{11,3},{4,12},{12,4},... | collective-permute-start | bytes 1572872 | tf_op jit(solution)/shard_map/ppermute | solution.py:340
  36.2 0.0 collective-permute-start
  36.2 0.0 copy-done
  36.2 0.1 dynamic-slice_bitcast_fusion.skip_ref
  36.3 2.2 %collective-permute-done.1.h_any = bf16[8,256,128]{2,1,0:T(8,128)(2,1)} collective-permute-done((bf16[8,256,128]{2,1,0:T(8,128)(2,1)}, bf16[8,256,128]{2,1,0:T(8,128)(2,1)}, u32[]{:S(2)}, u32[]{:S(2)}) %collective-permute-start.1) | collective-permute-done | bytes 524320 | tf_op jit(solution)/shard_map/ppermute | solution.py:340
  38.4 0.2 collective-permute-done.x_other
  38.7 7.1 %shard_map.97 = (bf16[4,256,128]{2,1,0:T(8,128)(2,1)S(1)}, bf16[4,256,128]{2,1,0:T(8,128)(2,1)S(1)}) custom-call(s32[1]{0:T(128)} %bitcast.core_ref, bf16[8,3,256,128]{3,2,1,0:T(8,128)(2,1)S(1)} %bitcast.16, bf16[8,256,128]{2,1,0:T(8,128)(2,1)S(1)} %collective-permute-done.x_other, bf16[8,256,128]{2,1,0:T(8,128)(2,1)} %collective-permute-done.1.h_any, ...), custom_call_target="tpu_custom_call" | custom-call | flops 1000000 | bytes 1048576 | tf_op jit(solution)/shard_map/pallas_call | solution.py:233
  45.8 0.0 copy-start.5
  45.8 0.0 copy-start.6
  45.8 0.5 collective-permute-start.2
  46.3 0.1 collective-permute-start.3
  46.4 1.0 %collective-permute-done.2.refs_2_ = bf16[4,256,128]{2,1,0:T(8,128)(2,1)S(1)} collective-permute-done((bf16[4,256,128]{2,1,0:T(8,128)(2,1)S(1)}, bf16[4,256,128]{2,1,0:T(8,128)(2,1)S(1)}, u32[]{:S(2)}, u32[]{:S(2)}) %collective-permute-start.2) | collective-permute-done | bytes 262176 | tf_op jit(solution)/shard_map/ppermute | solution.py:340
  47.5 0.0 copy-done.5
  47.5 0.0 copy-done.6
  47.5 0.4 collective-permute-done.3.refs_3_
  47.8 0.0 all-to-all-done.1
  47.9 2.4 %collective-permute-start.4 = (bf16[8,256,128]{2,1,0:T(8,128)(2,1)S(1)}, bf16[8,256,128]{2,1,0:T(8,128)(2,1)S(1)}, u32[]{:S(2)}, u32[]{:S(2)}) collective-permute-start(bf16[8,256,128]{2,1,0:T(8,128)(2,1)S(1)} %slice_bitcast_fusion), channel_id=1, source_target_pairs={{0,8},{8,0},{1,9},{9,1},{2,10},{10,2},{3,11},{11,3},{4,12},{12,4},... | collective-permute-start | bytes 1572872 | tf_op jit(solution)/shard_map/ppermute | solution.py:340
  50.3 1.5 %collective-permute-done.4.k_other = bf16[8,256,128]{2,1,0:T(8,128)(2,1)S(1)} collective-permute-done((bf16[8,256,128]{2,1,0:T(8,128)(2,1)S(1)}, bf16[8,256,128]{2,1,0:T(8,128)(2,1)S(1)}, u32[]{:S(2)}, u32[]{:S(2)}) %collective-permute-start.4) | collective-permute-done | bytes 524320 | tf_op jit(solution)/shard_map/ppermute | solution.py:340
  51.8 6.3 %shard_map.98 = bf16[8,2,256,128]{3,2,1,0:T(8,128)(2,1)S(1)} custom-call(s32[1]{0:T(128)} %bitcast.core_ref, bf16[8,2,256,128]{3,2,1,0:T(8,128)(2,1)S(1)} %bitcast.19, bf16[8,256,128]{2,1,0:T(8,128)(2,1)S(1)} %collective-permute-done.4.k_other, bf16[4,256,128]{2,1,0:T(8,128)(2,1)} %copy-done.5, bf16[4,256,128]{2,1,0:T(8,128)(2,1)} %copy-done.6, ...), custom_call_target="tpu_custom_call" | custom-call | flops 1000000000 | bytes 1048576 | tf_op jit(solution)/shard_map/pallas_call | solution.py:320
  58.1 18.0 %all_to_all.15 = bf16[8,512,128]{2,1,0:T(8,128)(2,1)S(1)} all-to-all(bf16[8,512,128]{2,1,0:T(8,128)(2,1)S(1)} %bitcast.21), channel_id=1, replica_groups=mesh['chip'=8,'core'=2,'tp'=8] {'chip'}, dimensions={0} | all-to-all | bytes 2097152 | tf_op jit(solution)/shard_map/all_to_all | solution.py:335
  76.1 1.1 %shard_map.99 = (bf16[256,1024]{1,0:T(8,128)(2,1)}, bf16[256,1024]{1,0:T(8,128)(2,1)}) custom-call(bf16[8,2,256,128]{3,2,1,0:T(8,128)(2,1)S(1)} %bitcast.17), custom_call_target="tpu_custom_call" | custom-call | bytes 2097152 | tf_op jit(solution)/shard_map/pallas_call | solution.py:141
  (1 shorter events, 0.0 us)
Async XLA Ops:
  0.6 35.6 %copy-start = (f32[1024]{0:T(1024)S(1)}, f32[1024]{0:T(1024)}, u32[]{:S(2)}) copy-start(f32[1024]{0:T(1024)} %param.11) | copy-start | bytes 12292
  3.2 6.1 %copy-start.2 = (bf16[256,1024]{1,0:T(8,128)(2,1)S(1)}, bf16[256,1024]{1,0:T(8,128)(2,1)}, u32[]{:S(2)}) copy-start(bf16[256,1024]{1,0:T(8,128)(2,1)} %queries.1) | copy-start | bytes 1572868
  3.2 26.5 %all-to-all-start = ((bf16[8,768,128]{2,1,0:T(8,128)(2,1)}), bf16[8,768,128]{2,1,0:T(8,128)(2,1)S(1)}, u32[]{:S(2)}, u32[]{:S(2)}) async-start(bf16[8,768,128]{2,1,0:T(8,128)(2,1)} %bitcast.1), calls=%async_computation | async-start | bytes 3145728 | tf_op jit(solution)/shard_map/all_to_all | solution.py:335
  9.3 1.0 %copy-start.3 = (bf16[256,1024]{1,0:T(8,128)(2,1)S(1)}, bf16[256,1024]{1,0:T(8,128)(2,1)}, u32[]{:S(2)}) copy-start(bf16[256,1024]{1,0:T(8,128)(2,1)} %keys.1) | copy-start | bytes 1572868
  10.3 0.9 %copy-start.4 = (bf16[512,256]{1,0:T(8,128)(2,1)S(1)}, bf16[512,256]{1,0:T(8,128)(2,1)}, u32[]{:S(2)}) copy-start(bf16[512,256]{1,0:T(8,128)(2,1)} %constant.21.clone.forward) | copy-start | bytes 786436
  11.5 1.0 %copy-start.1 = (bf16[8,2,256,128]{3,2,1,0:T(8,128)(2,1)}, bf16[8,2,256,128]{3,2,1,0:T(8,128)(2,1)S(1)}, u32[]{:S(2)}) copy-start(bf16[8,2,256,128]{3,2,1,0:T(8,128)(2,1)S(1)} %get-tuple-element.14) | copy-start | bytes 3145732
  29.7 18.1 %all-to-all-start.1 = ((bf16[8,512,128]{2,1,0:T(8,128)(2,1)}), bf16[8,512,128]{2,1,0:T(8,128)(2,1)S(1)}, u32[]{:S(2)}, u32[]{:S(2)}) async-start(bf16[8,512,128]{2,1,0:T(8,128)(2,1)} %bitcast.20), calls=%async_computation.1 | async-start | bytes 2097152 | tf_op jit(solution)/shard_map/all_to_all | solution.py:335
  34.5 3.9 %collective-permute-start.1 = (bf16[8,256,128]{2,1,0:T(8,128)(2,1)}, bf16[8,256,128]{2,1,0:T(8,128)(2,1)}, u32[]{:S(2)}, u32[]{:S(2)}) collective-permute-start(bf16[8,256,128]{2,1,0:T(8,128)(2,1)} %get-tuple-element.22), channel_id=1, source_target_pairs={{0,8},{8,0},{1,9},{9,1},{2,10},{10,2},{3,11},{11,3},{4,12},{12,4},... | collective-permute-start | bytes 1572872 | tf_op jit(solution)/shard_map/ppermute | solution.py:340
  36.2 2.5 %collective-permute-start = (bf16[8,256,128]{2,1,0:T(8,128)(2,1)}, bf16[8,256,128]{2,1,0:T(8,128)(2,1)S(1)}, u32[]{:S(2)}, u32[]{:S(2)}) collective-permute-start(bf16[8,256,128]{2,1,0:T(8,128)(2,1)} %get-tuple-element.23), channel_id=1, source_target_pairs={{0,8},{8,0},{1,9},{9,1},{2,10},{10,2},{3,11},{11,3},{4,12},{12,4},... | collective-permute-start | bytes 1572872 | tf_op jit(solution)/shard_map/ppermute | solution.py:340
  45.8 1.6 %copy-start.5 = (bf16[4,256,128]{2,1,0:T(8,128)(2,1)}, bf16[4,256,128]{2,1,0:T(8,128)(2,1)S(1)}, u32[]{:S(2)}) copy-start(bf16[4,256,128]{2,1,0:T(8,128)(2,1)S(1)} %get-tuple-element.17.refs_0_) | copy-start | bytes 786436
  45.8 1.6 %copy-start.6 = (bf16[4,256,128]{2,1,0:T(8,128)(2,1)}, bf16[4,256,128]{2,1,0:T(8,128)(2,1)S(1)}, u32[]{:S(2)}) copy-start(bf16[4,256,128]{2,1,0:T(8,128)(2,1)S(1)} %get-tuple-element.18.refs_1_) | copy-start | bytes 786436
  45.8 1.6 %collective-permute-start.2 = (bf16[4,256,128]{2,1,0:T(8,128)(2,1)S(1)}, bf16[4,256,128]{2,1,0:T(8,128)(2,1)S(1)}, u32[]{:S(2)}, u32[]{:S(2)}) collective-permute-start(bf16[4,256,128]{2,1,0:T(8,128)(2,1)S(1)} %get-tuple-element.17.refs_0_), channel_id=1, source_target_pairs={{0,8},{8,0},{1,9},{9,1},{2,10},{10,2},{3,11},{11,3},{4,12},{12,4},... | collective-permute-start | bytes 786440 | tf_op jit(solution)/shard_map/ppermute | solution.py:340
  46.3 1.5 %collective-permute-start.3 = (bf16[4,256,128]{2,1,0:T(8,128)(2,1)S(1)}, bf16[4,256,128]{2,1,0:T(8,128)(2,1)S(1)}, u32[]{:S(2)}, u32[]{:S(2)}) collective-permute-start(bf16[4,256,128]{2,1,0:T(8,128)(2,1)S(1)} %get-tuple-element.18.refs_1_), channel_id=1, source_target_pairs={{0,8},{8,0},{1,9},{9,1},{2,10},{10,2},{3,11},{11,3},{4,12},{12,4},... | collective-permute-start | bytes 786440 | tf_op jit(solution)/shard_map/ppermute | solution.py:340
  47.9 3.9 %collective-permute-start.4 = (bf16[8,256,128]{2,1,0:T(8,128)(2,1)S(1)}, bf16[8,256,128]{2,1,0:T(8,128)(2,1)S(1)}, u32[]{:S(2)}, u32[]{:S(2)}) collective-permute-start(bf16[8,256,128]{2,1,0:T(8,128)(2,1)S(1)} %slice_bitcast_fusion), channel_id=1, source_target_pairs={{0,8},{8,0},{1,9},{9,1},{2,10},{10,2},{3,11},{11,3},{4,12},{12,4},... | collective-permute-start | bytes 1572872 | tf_op jit(solution)/shard_map/ppermute | solution.py:340

commit v3 on v2

--- a/solution.py
+++ b/solution.py
@@ -250,84 +250,146 @@
     )(core, own, x_other, in_hbm(h_other), skip, forward, in_hbm(inverse))
 
 
-def attend_kernel(core_ref, qk_own, k_other, *refs):
-    v_any, v_other, refs = refs[:PARTS], refs[PARTS : 2 * PARTS], refs[2 * PARTS :]
-    out, v_own, v_sem = refs
+def dot(a, b):
+    return jnp.dot(a, b, preferred_element_type=jnp.float32)
+
+
+def scores(q, k):
+    return lax.dot_general(q, k, (((1,), (1,)), ((), ())), preferred_element_type=jnp.float32)
+
+
+def chunks(count):
+    return [(j, min(j + 2, count)) for j in range(0, count, 2)]
+
+
+def rows_of(blocks, span):
+    return jnp.concatenate([blocks[j][...] for j in range(*span)], axis=0)
+
+
+def with_ones(values):
+    return jnp.concatenate([values, jnp.ones(values.shape, values.dtype)], axis=1)
+
+
+def sweep(blocks, make_scores, values, begin, finish):
+    order = list(range(blocks))[::-1]
+    current = [make_scores(order[0], span) for span in chunks(order[0] + 1)]
+    for i, b in enumerate(order):
+        top = current[0].max(axis=1, keepdims=True)
+        for s in current[1:]:
+            top = jnp.maximum(top, s.max(axis=1, keepdims=True))
+        top, total = begin(b, top)
+        later = chunks(order[i + 1] + 1) if i + 1 < blocks else []
+        following = []
+        for n, span in enumerate(chunks(b + 1)):
+            if n < len(later):
+                following.append(make_scores(order[i + 1], later[n]))
+            s = current[n]
+            wide = jnp.concatenate([top] * (s.shape[1] // top.shape[1]), axis=1)
+            weights = jnp.exp2((s - wide) * TO_EXP2).astype(jnp.bfloat16)
+            part = dot(weights, with_ones(rows_of(values, span)))
+            total = part if total is None else total + part
+        finish(b, top, total)
+        current = following
+
+
+def own_kernel(qk_own, *refs):
+    v_any, refs = refs[:PARTS], refs[PARTS:]
+    total_ref, top_ref, v_own, v_sem = refs
     blocks, _, rows, lanes = qk_own.shape
     each = blocks // PARTS
-    values = [
+    loads = [
         pltpu.make_async_copy(part, v_own.at[pl.ds(i * each, each)], v_sem.at[i])
         for i, part in enumerate(v_any)
     ]
-    for c in values:
+    for c in loads:
         c.start()
-    core = core_ref[0]
     row = lax.broadcasted_iota(jnp.int32, (rows, rows), 0)
     col = lax.broadcasted_iota(jnp.int32, (rows, rows), 1)
     on_diagonal = col <= row
-    beside = jnp.full((rows, rows), core, jnp.int32) > 0
-    ones = jnp.ones((rows, lanes), jnp.bfloat16)
-
-    def product(q, k):
-        return lax.dot_general(
-            q, k, (((1,), (1,)), ((), ())), preferred_element_type=jnp.float32
-        )
-
-    def masked(b, j, s):
-        if j == b:
-            own = jnp.where(on_diagonal, s[:, :rows], MASKED)
-            other = jnp.where(beside, s[:, rows:], MASKED)
-            s = jnp.concatenate([own, other], axis=1)
-        return s
-
-    def scores(b, j):
-        both = jnp.concatenate([qk_own[j, 1], k_other[j]], axis=0)
-        return masked(b, j, product(qk_own[b, 0], both))
-
-    order = list(range(blocks))[::-1]
-    last = order[0]
-    current = [scores(last, j) for j in range(blocks)]
-    for c in values:
-        c.wait()
-    for i, b in enumerate(order):
-        top = current[0]
-        for s in current[1:]:
-            top = jnp.maximum(top, s)
-        top = jnp.max(top, axis=1, keepdims=True)
-        later = order[i + 1] if i + 1 < blocks else -1
-        following = []
-        total = None
-        for j in range(b + 1):
-            if j <= later:
-                following.append(scores(later, j))
-            weights = jnp.exp2((current[j] - top) * TO_EXP2).astype(jnp.bfloat16)
-            both = jnp.concatenate(
-                [
-                    jnp.concatenate([v_own[j], ones], axis=1),
-                    jnp.concatenate([v_other[j // each][j % each], ones], axis=1),
-                ],
-                axis=0,
-            )
-            part = jnp.dot(weights, both, preferred_element_type=jnp.float32)
-            total = part if total is None else total + part
-        out[b, 0] = v_own[b]
-        out[b, 1] = (total[:, :lanes] / total[:, lanes:]).astype(jnp.bfloat16)
-        current = following
-
-
-def attend(core, qk_own, k_other, v_own, v_other):
+
+    def make_scores(b, span):
+        parts = []
+        for j in range(*span):
+            s = scores(qk_own[b, 0], qk_own[j, 1])
+            parts.append(jnp.where(on_diagonal, s, MASKED) if j == b else s)
+        return jnp.concatenate(parts, axis=1)
+
+    def begin(b, top):
+        if b == blocks - 1:
+            for c in loads:
+                c.wait()
+        return jnp.broadcast_to(top, (rows, lanes)), None
+
+    def finish(b, top, total):
+        total_ref[b] = total
+        top_ref[b] = top
+
+    sweep(blocks, make_scores, [v_own.at[j] for j in range(blocks)], begin, finish)
+
+
+def attend_own(qk_own, v_own):
     blocks, _, rows, lanes = qk_own.shape
     return pl.pallas_call(
-        attend_kernel,
-        in_specs=[SMEM] + [VMEM] * 2 + [ANYWHERE] * PARTS + [VMEM] * PARTS,
-        out_specs=VMEM,
-        out_shape=jax.ShapeDtypeStruct((blocks, 2, rows, lanes), jnp.bfloat16),
+        own_kernel,
+        in_specs=[VMEM] + [ANYWHERE] * PARTS,
+        out_specs=[VMEM] * 2,
+        out_shape=[
+            jax.ShapeDtypeStruct((blocks, rows, 2 * lanes), jnp.float32),
+            jax.ShapeDtypeStruct((blocks, rows, lanes), jnp.float32),
+        ],
         scratch_shapes=[
             pltpu.VMEM((blocks, rows, lanes), jnp.bfloat16),
             pltpu.SemaphoreType.DMA((PARTS,)),
         ],
         **room(24, 10**9, MIB),
-    )(core, qk_own, k_other, *[in_hbm(v) for v in v_own], *v_other)
+    )(qk_own, *[in_hbm(v) for v in v_own])
+
+
+def other_kernel(core_ref, qk_own, k_other, total_ref, top_ref, *refs):
+    v_any, v_other, refs = refs[:PARTS], refs[PARTS : 2 * PARTS], refs[2 * PARTS :]
+    out, v_sem = refs
+    blocks, _, rows, lanes = qk_own.shape
+    each = blocks // PARTS
+    stores = [
+        pltpu.make_async_copy(part, out.at[pl.ds(i * each, each), 0], v_sem.at[i])
+        for i, part in enumerate(v_any)
+    ]
+    for c in stores:
+        c.start()
+    beside = jnp.full((rows, rows), core_ref[0], jnp.int32) > 0
+
+    def make_scores(b, span):
+        parts = []
+        for j in range(*span):
+            s = scores(qk_own[b, 0], k_other[j])
+            parts.append(jnp.where(beside, s, MASKED) if j == b else s)
+        return jnp.concatenate(parts, axis=1)
+
+    def begin(b, top):
+        before = top_ref[b]
+        top = jnp.maximum(before, top)
+        shrink = jnp.exp2((before - top) * TO_EXP2)
+        return top, total_ref[b] * jnp.concatenate([shrink, shrink], axis=1)
+
+    def finish(b, top, total):
+        out[b, 1] = (total[:, :lanes] / total[:, lanes:]).astype(jnp.bfloat16)
+
+    values = [v_other[j // each].at[j % each] for j in range(blocks)]
+    sweep(blocks, make_scores, values, begin, finish)
+    for c in stores:
+        c.wait()
+
+
+def attend_other(core, qk_own, k_other, total, top, v_own, v_other):
+    blocks, _, rows, lanes = qk_own.shape
+    return pl.pallas_call(
+        other_kernel,
+        in_specs=[SMEM] + [VMEM] * 4 + [ANYWHERE] * PARTS + [VMEM] * PARTS,
+        out_specs=VMEM,
+        out_shape=jax.ShapeDtypeStruct((blocks, 2, rows, lanes), jnp.bfloat16),
+        scratch_shapes=[pltpu.SemaphoreType.DMA((PARTS,))],
+        **room(24, 10**9, MIB),
+    )(core, qk_own, k_other, total, top, *[in_hbm(v) for v in v_own], *v_other)
 
 
 def to_chips(array):
@@ -353,7 +415,8 @@
     v_own = convolve(core, own, x_other, h_other, skip, packed[1], inverse)
     qk_own, v_other = lax.optimization_barrier((qk_own, [swap(v) for v in v_own]))
     k_other = swap(qk_own[:, 1])
-    back = to_chips(attend(core, qk_own, k_other, v_own, v_other))
+    total, top = attend_own(qk_own, v_own)
+    back = to_chips(attend_other(core, qk_own, k_other, total, top, v_own, v_other))
     mixed, attended = unpack(back)
     return (mixed, attended)
 

time: 78.1 us -> 77.3 us (0.990)
  local copies, waits for them, and re-layouts: 4.15 us -> 2.17 us
    unnamed x14, local copies, waits for them, and re-layouts: 3 us -> 1.02 us
    all_to_all x2, waiting for transfers between devices: 17.3 us -> 19.2 us  [to_chips(): lax.all_to_all(flat, 'chip', split_axis=0, concat_axis=0, tiled=True)]
    ppermute x5, waiting for transfers between devices: 5.35 us -> 3.81 us  [swap(): return lax.ppermute(array, 'core', [(0, 1), (1, 0)])]
    pallas_call x1 -> x2, Pallas kernels: 6.3 us -> 7.02 us  [the longest x1 3.82 us: attend_own(): pl.pallas_call(own_kernel, in_specs=[VMEM] + [ANYWHERE] * PARTS, out_spec...]
  transfers between devices with their start and end apart: 7 -> 7, of which waited for: 6 -> 5; matrix products, arithmetic and copies ran while one was open for 1% -> 1% of each run, Pallas kernels for 9% -> 14%
where the time goes in v3:
time: 77.3 us; the launch traced here: 77 us
  waiting for transfers between devices  23 us (30%)
  blocking collectives  18.6 us (24%)
  Pallas kernels  17.9 us (23%)
  starting transfers between devices  14.5 us (19%)
  local copies, waits for them, and re-layouts  2.17 us (3%)
    all_to_all x2, waiting for transfers between devices, to_chips(): lax.all_to_all(flat, 'chip', split_axis=0, concat_axis=0, tiled=True)  19.2 us
    all_to_all x1, blocking collectives, to_chips(): lax.all_to_all(flat, 'chip', split_axis=0, concat_axis=0, tiled=True)  18.6 us
    all_to_all x2, starting transfers between devices, to_chips(): lax.all_to_all(flat, 'chip', split_axis=0, concat_axis=0, tiled=True)  9.87 us
    pallas_call x1, Pallas kernels, convolve(): pl.pallas_call(conv_kernel, in_specs=[SMEM, VMEM, VMEM, ANYWHERE, VMEM, V...  7.13 us
    ppermute x5, starting transfers between devices, swap(): return lax.ppermute(array, 'core', [(0, 1), (1, 0)])  4.63 us
    pallas_call x1, Pallas kernels, attend_own(): pl.pallas_call(own_kernel, in_specs=[VMEM] + [ANYWHERE] * PARTS, out_spec...  3.82 us
    ppermute x5, waiting for transfers between devices, swap(): return lax.ppermute(array, 'core', [(0, 1), (1, 0)])  3.81 us
    pallas_call x1, Pallas kernels, attend_other(): pl.pallas_call(other_kernel, in_specs=[SMEM] + [VMEM] * 4 + [ANYWHERE] *...  3.21 us
  transfers between devices with their start and end apart: 7, of which 5 were waited for; matrix products, arithmetic and copies ran while one was open for 1% of the time, Pallas kernels for 14%

profile of v3, /device:TPU:1, one launch (start us, length us, event | category | flops | bytes accessed | tf_op | source)
XLA Modules:
  0.0 77.0 jit_solution(17572663174060569873)
XLA Ops:
  0.6 0.0 copy-start
  0.6 2.5 %shard_map.95 = bf16[8,3,256,128]{3,2,1,0:T(8,128)(2,1)} custom-call(bf16[256,1024]{1,0:T(8,128)(2,1)} %refs_0_.1, f32[256,1024]{1,0:T(8,128)} %refs_1_.1, bf16[256,1024]{1,0:T(8,128)(2,1)} %refs_2_.1), custom_call_target="tpu_custom_call" | custom-call | bytes 6291456 | tf_op jit(solution)/shard_map/pallas_call | solution.py:91
  3.1 0.0 copy-start.2
  3.1 0.0 copy-start.3
  3.2 0.0 copy-start.6
  3.2 6.1 %all-to-all-start = ((bf16[8,768,128]{2,1,0:T(8,128)(2,1)}), bf16[8,768,128]{2,1,0:T(8,128)(2,1)S(1)}, u32[]{:S(2)}, u32[]{:S(2)}) async-start(bf16[8,768,128]{2,1,0:T(8,128)(2,1)} %bitcast.1), calls=%async_computation | async-start | bytes 3145728 | tf_op jit(solution)/shard_map/all_to_all | solution.py:397
  9.3 0.0 copy-done.2
  9.3 0.0 copy-done.3
  9.3 0.0 copy-done.6
  9.3 0.2 shard_map.96
  9.5 0.0 copy-start.1
  9.5 1.0 %copy-done.1 = bf16[8,2,256,128]{3,2,1,0:T(8,128)(2,1)} copy-done((bf16[8,2,256,128]{3,2,1,0:T(8,128)(2,1)}, bf16[8,2,256,128]{3,2,1,0:T(8,128)(2,1)S(1)}, u32[]{:S(2)}) %copy-start.1) | copy-done | bytes 1048600
  10.5 19.2 %all-to-all-done = bf16[8,768,128]{2,1,0:T(8,128)(2,1)S(1)} async-done(((bf16[8,768,128]{2,1,0:T(8,128)(2,1)}), bf16[8,768,128]{2,1,0:T(8,128)(2,1)S(1)}, u32[]{:S(2)}, u32[]{:S(2)}) %all-to-all-start) | async-done | bytes 1572896 | tf_op jit(solution)/shard_map/all_to_all | solution.py:397
  29.7 3.8 %all-to-all-start.1 = ((bf16[8,512,128]{2,1,0:T(8,128)(2,1)}), bf16[8,512,128]{2,1,0:T(8,128)(2,1)S(1)}, u32[]{:S(2)}, u32[]{:S(2)}) async-start(bf16[8,512,128]{2,1,0:T(8,128)(2,1)} %bitcast.22), calls=%async_computation.1 | async-start | bytes 2097152 | tf_op jit(solution)/shard_map/all_to_all | solution.py:397
  33.5 1.0 %slice_bitcast_fusion.1 = (bf16[8,256,128]{2,1,0:T(8,128)(2,1)}, bf16[8,256,128]{2,1,0:T(8,128)(2,1)}) fusion(bf16[8,3,256,128]{3,2,1,0:T(8,128)(2,1)S(1)} %bitcast.15), kind=kLoop, calls=%fused_computation.1 | loop fusion | bytes 2097152 | tf_op jit(solution)/shard_map/squeeze | solution.py:413
  34.5 1.6 %collective-permute-start.1 = (bf16[8,256,128]{2,1,0:T(8,128)(2,1)}, bf16[8,256,128]{2,1,0:T(8,128)(2,1)}, u32[]{:S(2)}, u32[]{:S(2)}) collective-permute-start(bf16[8,256,128]{2,1,0:T(8,128)(2,1)} %get-tuple-element.26), channel_id=1, source_target_pairs={{0,8},{8,0},{1,9},{9,1},{2,10},{10,2},{3,11},{11,3},{4,12},{12,4},... | collective-permute-start | bytes 1572872 | tf_op jit(solution)/shard_map/ppermute | solution.py:402
  36.2 0.0 collective-permute-start
  36.2 0.0 copy-done
  36.2 0.1 dynamic-slice_bitcast_fusion.skip_ref
  36.3 2.2 %collective-permute-done.1.h_any = bf16[8,256,128]{2,1,0:T(8,128)(2,1)} collective-permute-done((bf16[8,256,128]{2,1,0:T(8,128)(2,1)}, bf16[8,256,128]{2,1,0:T(8,128)(2,1)}, u32[]{:S(2)}, u32[]{:S(2)}) %collective-permute-start.1) | collective-permute-done | bytes 524320 | tf_op jit(solution)/shard_map/ppermute | solution.py:402
  38.4 0.2 collective-permute-done.x_other
  38.7 7.1 %shard_map.97 = (bf16[4,256,128]{2,1,0:T(8,128)(2,1)S(1)}, bf16[4,256,128]{2,1,0:T(8,128)(2,1)S(1)}) custom-call(s32[1]{0:T(128)} %bitcast.core_ref, bf16[8,3,256,128]{3,2,1,0:T(8,128)(2,1)S(1)} %bitcast.16, bf16[8,256,128]{2,1,0:T(8,128)(2,1)S(1)} %collective-permute-done.x_other, bf16[8,256,128]{2,1,0:T(8,128)(2,1)} %collective-permute-done.1.h_any, ...), custom_call_target="tpu_custom_call" | custom-call | flops 1000000 | bytes 1048576 | tf_op jit(solution)/shard_map/pallas_call | solution.py:233
  45.8 0.0 copy-start.4
  45.8 0.0 copy-start.5
  45.8 0.5 collective-permute-start.2
  46.3 0.1 collective-permute-start.3
  46.4 1.0 %collective-permute-done.2.refs_2_ = bf16[4,256,128]{2,1,0:T(8,128)(2,1)S(1)} collective-permute-done((bf16[4,256,128]{2,1,0:T(8,128)(2,1)S(1)}, bf16[4,256,128]{2,1,0:T(8,128)(2,1)S(1)}, u32[]{:S(2)}, u32[]{:S(2)}) %collective-permute-start.2) | collective-permute-done | bytes 262176 | tf_op jit(solution)/shard_map/ppermute | solution.py:402
  47.5 0.0 copy-done.4
  47.5 0.0 copy-done.5
  47.5 0.4 collective-permute-done.3.refs_3_
  47.8 0.0 all-to-all-done.1
  47.9 2.4 %collective-permute-start.4 = (bf16[8,256,128]{2,1,0:T(8,128)(2,1)S(1)}, bf16[8,256,128]{2,1,0:T(8,128)(2,1)S(1)}, u32[]{:S(2)}, u32[]{:S(2)}) collective-permute-start(bf16[8,256,128]{2,1,0:T(8,128)(2,1)S(1)} %slice_bitcast_fusion), channel_id=1, source_target_pairs={{0,8},{8,0},{1,9},{9,1},{2,10},{10,2},{3,11},{11,3},{4,12},{12,4},... | collective-permute-start | bytes 1572872 | tf_op jit(solution)/shard_map/ppermute | solution.py:402
  50.3 3.8 %shard_map.98 = (f32[8,256,256]{2,1,0:T(8,128)S(1)}, f32[8,256,128]{2,1,0:T(8,128)S(1)}) custom-call(bf16[8,2,256,128]{3,2,1,0:T(8,128)(2,1)S(1)} %bitcast.18, bf16[4,256,128]{2,1,0:T(8,128)(2,1)} %copy-done.4, bf16[4,256,128]{2,1,0:T(8,128)(2,1)} %copy-done.5), custom_call_target="tpu_custom_call" | custom-call | flops 1000000000 | bytes 1048576 | tf_op jit(solution)/shard_map/pallas_call | solution.py:332
  54.1 0.0 collective-permute-done.4.k_other
  54.1 3.2 %shard_map.99 = bf16[8,2,256,128]{3,2,1,0:T(8,128)(2,1)S(1)} custom-call(s32[1]{0:T(128)} %bitcast.core_ref, bf16[8,2,256,128]{3,2,1,0:T(8,128)(2,1)S(1)} %bitcast.19, bf16[8,256,128]{2,1,0:T(8,128)(2,1)S(1)} %collective-permute-done.4.k_other, f32[8,256,256]{2,1,0:T(8,128)S(1)} %get-tuple-element.22.total_ref, ...), custom_call_target="tpu_custom_call" | custom-call | flops 1000000000 | bytes 1048576 | tf_op jit(solution)/shard_map/pallas_call | solution.py:385
  57.3 18.6 %all_to_all.15 = bf16[8,512,128]{2,1,0:T(8,128)(2,1)S(1)} all-to-all(bf16[8,512,128]{2,1,0:T(8,128)(2,1)S(1)} %bitcast.21), channel_id=1, replica_groups=mesh['chip'=8,'core'=2,'tp'=8] {'chip'}, dimensions={0} | all-to-all | bytes 2097152 | tf_op jit(solution)/shard_map/all_to_all | solution.py:397
  75.9 1.1 %shard_map.100 = (bf16[256,1024]{1,0:T(8,128)(2,1)}, bf16[256,1024]{1,0:T(8,128)(2,1)}) custom-call(bf16[8,2,256,128]{3,2,1,0:T(8,128)(2,1)S(1)} %bitcast.20), custom_call_target="tpu_custom_call" | custom-call | bytes 2097152 | tf_op jit(solution)/shard_map/pallas_call | solution.py:141
  (1 shorter events, 0.0 us)
Async XLA Ops:
  0.6 35.6 %copy-start = (f32[1024]{0:T(1024)S(1)}, f32[1024]{0:T(1024)}, u32[]{:S(2)}) copy-start(f32[1024]{0:T(1024)} %param.11) | copy-start | bytes 12292
  3.1 6.1 %copy-start.2 = (bf16[256,1024]{1,0:T(8,128)(2,1)S(1)}, bf16[256,1024]{1,0:T(8,128)(2,1)}, u32[]{:S(2)}) copy-start(bf16[256,1024]{1,0:T(8,128)(2,1)} %queries.1) | copy-start | bytes 1572868
  3.1 6.1 %copy-start.3 = (bf16[256,1024]{1,0:T(8,128)(2,1)S(1)}, bf16[256,1024]{1,0:T(8,128)(2,1)}, u32[]{:S(2)}) copy-start(bf16[256,1024]{1,0:T(8,128)(2,1)} %keys.1) | copy-start | bytes 1572868
  3.2 6.1 %copy-start.6 = (bf16[512,256]{1,0:T(8,128)(2,1)S(1)}, bf16[512,256]{1,0:T(8,128)(2,1)}, u32[]{:S(2)}) copy-start(bf16[512,256]{1,0:T(8,128)(2,1)} %constant.21.clone.forward) | copy-start | bytes 786436
  3.2 26.5 %all-to-all-start = ((bf16[8,768,128]{2,1,0:T(8,128)(2,1)}), bf16[8,768,128]{2,1,0:T(8,128)(2,1)S(1)}, u32[]{:S(2)}, u32[]{:S(2)}) async-start(bf16[8,768,128]{2,1,0:T(8,128)(2,1)} %bitcast.1), calls=%async_computation | async-start | bytes 3145728 | tf_op jit(solution)/shard_map/all_to_all | solution.py:397
  9.5 1.0 %copy-start.1 = (bf16[8,2,256,128]{3,2,1,0:T(8,128)(2,1)}, bf16[8,2,256,128]{3,2,1,0:T(8,128)(2,1)S(1)}, u32[]{:S(2)}) copy-start(bf16[8,2,256,128]{3,2,1,0:T(8,128)(2,1)S(1)} %get-tuple-element.16) | copy-start | bytes 3145732
  29.7 18.1 %all-to-all-start.1 = ((bf16[8,512,128]{2,1,0:T(8,128)(2,1)}), bf16[8,512,128]{2,1,0:T(8,128)(2,1)S(1)}, u32[]{:S(2)}, u32[]{:S(2)}) async-start(bf16[8,512,128]{2,1,0:T(8,128)(2,1)} %bitcast.22), calls=%async_computation.1 | async-start | bytes 2097152 | tf_op jit(solution)/shard_map/all_to_all | solution.py:397
  34.5 3.9 %collective-permute-start.1 = (bf16[8,256,128]{2,1,0:T(8,128)(2,1)}, bf16[8,256,128]{2,1,0:T(8,128)(2,1)}, u32[]{:S(2)}, u32[]{:S(2)}) collective-permute-start(bf16[8,256,128]{2,1,0:T(8,128)(2,1)} %get-tuple-element.26), channel_id=1, source_target_pairs={{0,8},{8,0},{1,9},{9,1},{2,10},{10,2},{3,11},{11,3},{4,12},{12,4},... | collective-permute-start | bytes 1572872 | tf_op jit(solution)/shard_map/ppermute | solution.py:402
  36.2 2.5 %collective-permute-start = (bf16[8,256,128]{2,1,0:T(8,128)(2,1)}, bf16[8,256,128]{2,1,0:T(8,128)(2,1)S(1)}, u32[]{:S(2)}, u32[]{:S(2)}) collective-permute-start(bf16[8,256,128]{2,1,0:T(8,128)(2,1)} %get-tuple-element.27), channel_id=1, source_target_pairs={{0,8},{8,0},{1,9},{9,1},{2,10},{10,2},{3,11},{11,3},{4,12},{12,4},... | collective-permute-start | bytes 1572872 | tf_op jit(solution)/shard_map/ppermute | solution.py:402
  45.8 1.6 %copy-start.4 = (bf16[4,256,128]{2,1,0:T(8,128)(2,1)}, bf16[4,256,128]{2,1,0:T(8,128)(2,1)S(1)}, u32[]{:S(2)}) copy-start(bf16[4,256,128]{2,1,0:T(8,128)(2,1)S(1)} %get-tuple-element.19.refs_0_) | copy-start | bytes 786436
  45.8 1.6 %copy-start.5 = (bf16[4,256,128]{2,1,0:T(8,128)(2,1)}, bf16[4,256,128]{2,1,0:T(8,128)(2,1)S(1)}, u32[]{:S(2)}) copy-start(bf16[4,256,128]{2,1,0:T(8,128)(2,1)S(1)} %get-tuple-element.20.refs_1_) | copy-start | bytes 786436
  45.8 1.6 %collective-permute-start.2 = (bf16[4,256,128]{2,1,0:T(8,128)(2,1)S(1)}, bf16[4,256,128]{2,1,0:T(8,128)(2,1)S(1)}, u32[]{:S(2)}, u32[]{:S(2)}) collective-permute-start(bf16[4,256,128]{2,1,0:T(8,128)(2,1)S(1)} %get-tuple-element.19.refs_0_), channel_id=1, source_target_pairs={{0,8},{8,0},{1,9},{9,1},{2,10},{10,2},{3,11},{11,3},{4,12},{12,4},... | collective-permute-start | bytes 786440 | tf_op jit(solution)/shard_map/ppermute | solution.py:402
  46.3 1.5 %collective-permute-start.3 = (bf16[4,256,128]{2,1,0:T(8,128)(2,1)S(1)}, bf16[4,256,128]{2,1,0:T(8,128)(2,1)S(1)}, u32[]{:S(2)}, u32[]{:S(2)}) collective-permute-start(bf16[4,256,128]{2,1,0:T(8,128)(2,1)S(1)} %get-tuple-element.20.refs_1_), channel_id=1, source_target_pairs={{0,8},{8,0},{1,9},{9,1},{2,10},{10,2},{3,11},{11,3},{4,12},{12,4},... | collective-permute-start | bytes 786440 | tf_op jit(solution)/shard_map/ppermute | solution.py:402
  47.9 6.2 %collective-permute-start.4 = (bf16[8,256,128]{2,1,0:T(8,128)(2,1)S(1)}, bf16[8,256,128]{2,1,0:T(8,128)(2,1)S(1)}, u32[]{:S(2)}, u32[]{:S(2)}) collective-permute-start(bf16[8,256,128]{2,1,0:T(8,128)(2,1)S(1)} %slice_bitcast_fusion), channel_id=1, source_target_pairs={{0,8},{8,0},{1,9},{9,1},{2,10},{10,2},{3,11},{11,3},{4,12},{12,4},... | collective-permute-start | bytes 1572872 | tf_op jit(solution)/shard_map/ppermute | solution.py:402

commit v4 on v3

--- a/solution.py
+++ b/solution.py
@@ -86,7 +86,7 @@
     rows, channels = arrays[0].shape
     chips = channels // HEAD_DIM
     count = len(arrays)
-    parts = 4
+    parts = 2
     shape = (chips, count, rows, HEAD_DIM)
     return pl.pallas_call(
         functools.partial(pack_kernel, count=count, parts=parts),
@@ -270,16 +270,19 @@
     return jnp.concatenate([values, jnp.ones(values.shape, values.dtype)], axis=1)
 
 
-def sweep(blocks, make_scores, values, begin, finish):
+def sweep(blocks, make_scores, values, begin, finish, ahead=0):
     order = list(range(blocks))[::-1]
     current = [make_scores(order[0], span) for span in chunks(order[0] + 1)]
+    early = [make_scores(b, span) for b in order[1 : 1 + ahead] for span in chunks(b + 1)]
     for i, b in enumerate(order):
         top = current[0].max(axis=1, keepdims=True)
         for s in current[1:]:
             top = jnp.maximum(top, s.max(axis=1, keepdims=True))
         top, total = begin(b, top)
         later = chunks(order[i + 1] + 1) if i + 1 < blocks else []
-        following = []
+        following = early[: len(later)] if i < ahead else []
+        early = early[len(later) :] if i < ahead else []
+        later = [] if i < ahead else later
         for n, span in enumerate(chunks(b + 1)):
             if n < len(later):
                 following.append(make_scores(order[i + 1], later[n]))
@@ -324,7 +327,7 @@
         total_ref[b] = total
         top_ref[b] = top
 
-    sweep(blocks, make_scores, [v_own.at[j] for j in range(blocks)], begin, finish)
+    sweep(blocks, make_scores, [v_own.at[j] for j in range(blocks)], begin, finish, 1)
 
 
 def attend_own(qk_own, v_own):

time: 77.3 us -> 76.9 us (level)
  no operation moved by 1% of the time
where the time goes in v4:
time: 76.9 us; the launch traced here: 76.6 us
  waiting for transfers between devices  23 us (30%)
  blocking collectives  18.6 us (24%)
  Pallas kernels  17.5 us (23%)
  starting transfers between devices  14.5 us (19%)
  local copies, waits for them, and re-layouts  2.17 us (3%)
  between operations  0.77 us (1%)
    all_to_all x2, waiting for transfers between devices, to_chips(): lax.all_to_all(flat, 'chip', split_axis=0, concat_axis=0, tiled=True)  19.2 us
    all_to_all x1, blocking collectives, to_chips(): lax.all_to_all(flat, 'chip', split_axis=0, concat_axis=0, tiled=True)  18.6 us
    all_to_all x2, starting transfers between devices, to_chips(): lax.all_to_all(flat, 'chip', split_axis=0, concat_axis=0, tiled=True)  9.87 us
    pallas_call x1, Pallas kernels, convolve(): pl.pallas_call(conv_kernel, in_specs=[SMEM, VMEM, VMEM, ANYWHERE, VMEM, V...  7.13 us
    ppermute x5, starting transfers between devices, swap(): return lax.ppermute(array, 'core', [(0, 1), (1, 0)])  4.63 us
    ppermute x5, waiting for transfers between devices, swap(): return lax.ppermute(array, 'core', [(0, 1), (1, 0)])  3.81 us
    pallas_call x1, Pallas kernels, attend_own(): pl.pallas_call(own_kernel, in_specs=[VMEM] + [ANYWHERE] * PARTS, out_spec...  3.51 us
    pallas_call x1, Pallas kernels, attend_other(): pl.pallas_call(other_kernel, in_specs=[SMEM] + [VMEM] * 4 + [ANYWHERE] *...  3.21 us
  transfers between devices with their start and end apart: 7, of which 5 were waited for; matrix products, arithmetic and copies ran while one was open for 1% of the time, Pallas kernels for 14%

profile of v4, /device:TPU:1, one launch (start us, length us, event | category | flops | bytes accessed | tf_op | source)
XLA Modules:
  0.0 76.6 jit_solution(4944603287885617148)
XLA Ops:
  0.6 0.0 copy-start
  0.6 2.4 %shard_map.95 = bf16[8,3,256,128]{3,2,1,0:T(8,128)(2,1)} custom-call(bf16[256,1024]{1,0:T(8,128)(2,1)} %refs_0_.1, f32[256,1024]{1,0:T(8,128)} %refs_1_.1, bf16[256,1024]{1,0:T(8,128)(2,1)} %refs_2_.1), custom_call_target="tpu_custom_call" | custom-call | bytes 6291456 | tf_op jit(solution)/shard_map/pallas_call | solution.py:91
  3.0 0.0 copy-start.2
  3.0 0.0 copy-start.3
  3.0 0.0 copy-start.6
  3.1 6.1 %all-to-all-start = ((bf16[8,768,128]{2,1,0:T(8,128)(2,1)}), bf16[8,768,128]{2,1,0:T(8,128)(2,1)S(1)}, u32[]{:S(2)}, u32[]{:S(2)}) async-start(bf16[8,768,128]{2,1,0:T(8,128)(2,1)} %bitcast.1), calls=%async_computation | async-start | bytes 3145728 | tf_op jit(solution)/shard_map/all_to_all | solution.py:400
  9.2 0.0 copy-done.2
  9.2 0.0 copy-done.3
  9.2 0.0 copy-done.6
  9.2 0.2 shard_map.96
  9.4 0.0 copy-start.1
  9.4 1.0 %copy-done.1 = bf16[8,2,256,128]{3,2,1,0:T(8,128)(2,1)} copy-done((bf16[8,2,256,128]{3,2,1,0:T(8,128)(2,1)}, bf16[8,2,256,128]{3,2,1,0:T(8,128)(2,1)S(1)}, u32[]{:S(2)}) %copy-start.1) | copy-done | bytes 1048600
  10.4 19.2 %all-to-all-done = bf16[8,768,128]{2,1,0:T(8,128)(2,1)S(1)} async-done(((bf16[8,768,128]{2,1,0:T(8,128)(2,1)}), bf16[8,768,128]{2,1,0:T(8,128)(2,1)S(1)}, u32[]{:S(2)}, u32[]{:S(2)}) %all-to-all-start) | async-done | bytes 1572896 | tf_op jit(solution)/shard_map/all_to_all | solution.py:400
  29.6 3.8 %all-to-all-start.1 = ((bf16[8,512,128]{2,1,0:T(8,128)(2,1)}), bf16[8,512,128]{2,1,0:T(8,128)(2,1)S(1)}, u32[]{:S(2)}, u32[]{:S(2)}) async-start(bf16[8,512,128]{2,1,0:T(8,128)(2,1)} %bitcast.22), calls=%async_computation.1 | async-start | bytes 2097152 | tf_op jit(solution)/shard_map/all_to_all | solution.py:400
  33.4 1.0 %slice_bitcast_fusion.1 = (bf16[8,256,128]{2,1,0:T(8,128)(2,1)}, bf16[8,256,128]{2,1,0:T(8,128)(2,1)}) fusion(bf16[8,3,256,128]{3,2,1,0:T(8,128)(2,1)S(1)} %bitcast.15), kind=kLoop, calls=%fused_computation.1 | loop fusion | bytes 2097152 | tf_op jit(solution)/shard_map/squeeze | solution.py:416
  34.4 1.6 %collective-permute-start.1 = (bf16[8,256,128]{2,1,0:T(8,128)(2,1)}, bf16[8,256,128]{2,1,0:T(8,128)(2,1)}, u32[]{:S(2)}, u32[]{:S(2)}) collective-permute-start(bf16[8,256,128]{2,1,0:T(8,128)(2,1)} %get-tuple-element.26), channel_id=1, source_target_pairs={{0,8},{8,0},{1,9},{9,1},{2,10},{10,2},{3,11},{11,3},{4,12},{12,4},... | collective-permute-start | bytes 1572872 | tf_op jit(solution)/shard_map/ppermute | solution.py:405
  36.1 0.0 collective-permute-start
  36.1 0.0 copy-done
  36.1 0.1 dynamic-slice_bitcast_fusion.skip_ref
  36.2 2.2 %collective-permute-done.1.h_any = bf16[8,256,128]{2,1,0:T(8,128)(2,1)} collective-permute-done((bf16[8,256,128]{2,1,0:T(8,128)(2,1)}, bf16[8,256,128]{2,1,0:T(8,128)(2,1)}, u32[]{:S(2)}, u32[]{:S(2)}) %collective-permute-start.1) | collective-permute-done | bytes 524320 | tf_op jit(solution)/shard_map/ppermute | solution.py:405
  38.3 0.2 collective-permute-done.x_other
  38.6 7.1 %shard_map.97 = (bf16[4,256,128]{2,1,0:T(8,128)(2,1)S(1)}, bf16[4,256,128]{2,1,0:T(8,128)(2,1)S(1)}) custom-call(s32[1]{0:T(128)} %bitcast.core_ref, bf16[8,3,256,128]{3,2,1,0:T(8,128)(2,1)S(1)} %bitcast.16, bf16[8,256,128]{2,1,0:T(8,128)(2,1)S(1)} %collective-permute-done.x_other, bf16[8,256,128]{2,1,0:T(8,128)(2,1)} %collective-permute-done.1.h_any, ...), custom_call_target="tpu_custom_call" | custom-call | flops 1000000 | bytes 1048576 | tf_op jit(solution)/shard_map/pallas_call | solution.py:233
  45.7 0.0 copy-start.4
  45.7 0.0 copy-start.5
  45.7 0.5 collective-permute-start.2
  46.2 0.1 collective-permute-start.3
  46.3 1.0 %collective-permute-done.2.refs_2_ = bf16[4,256,128]{2,1,0:T(8,128)(2,1)S(1)} collective-permute-done((bf16[4,256,128]{2,1,0:T(8,128)(2,1)S(1)}, bf16[4,256,128]{2,1,0:T(8,128)(2,1)S(1)}, u32[]{:S(2)}, u32[]{:S(2)}) %collective-permute-start.2) | collective-permute-done | bytes 262176 | tf_op jit(solution)/shard_map/ppermute | solution.py:405
  47.4 0.0 copy-done.4
  47.4 0.0 copy-done.5
  47.4 0.4 collective-permute-done.3.refs_3_
  47.7 0.0 all-to-all-done.1
  47.8 2.4 %collective-permute-start.4 = (bf16[8,256,128]{2,1,0:T(8,128)(2,1)S(1)}, bf16[8,256,128]{2,1,0:T(8,128)(2,1)S(1)}, u32[]{:S(2)}, u32[]{:S(2)}) collective-permute-start(bf16[8,256,128]{2,1,0:T(8,128)(2,1)S(1)} %slice_bitcast_fusion), channel_id=1, source_target_pairs={{0,8},{8,0},{1,9},{9,1},{2,10},{10,2},{3,11},{11,3},{4,12},{12,4},... | collective-permute-start | bytes 1572872 | tf_op jit(solution)/shard_map/ppermute | solution.py:405
  50.2 3.5 %shard_map.98 = (f32[8,256,256]{2,1,0:T(8,128)S(1)}, f32[8,256,128]{2,1,0:T(8,128)S(1)}) custom-call(bf16[8,2,256,128]{3,2,1,0:T(8,128)(2,1)S(1)} %bitcast.18, bf16[4,256,128]{2,1,0:T(8,128)(2,1)} %copy-done.4, bf16[4,256,128]{2,1,0:T(8,128)(2,1)} %copy-done.5), custom_call_target="tpu_custom_call" | custom-call | flops 1000000000 | bytes 1048576 | tf_op jit(solution)/shard_map/pallas_call | solution.py:335
  53.7 0.0 collective-permute-done.4.k_other
  53.7 3.2 %shard_map.99 = bf16[8,2,256,128]{3,2,1,0:T(8,128)(2,1)S(1)} custom-call(s32[1]{0:T(128)} %bitcast.core_ref, bf16[8,2,256,128]{3,2,1,0:T(8,128)(2,1)S(1)} %bitcast.19, bf16[8,256,128]{2,1,0:T(8,128)(2,1)S(1)} %collective-permute-done.4.k_other, f32[8,256,256]{2,1,0:T(8,128)S(1)} %get-tuple-element.22.total_ref, ...), custom_call_target="tpu_custom_call" | custom-call | flops 1000000000 | bytes 1048576 | tf_op jit(solution)/shard_map/pallas_call | solution.py:388
  56.9 18.6 %all_to_all.15 = bf16[8,512,128]{2,1,0:T(8,128)(2,1)S(1)} all-to-all(bf16[8,512,128]{2,1,0:T(8,128)(2,1)S(1)} %bitcast.21), channel_id=1, replica_groups=mesh['chip'=8,'core'=2,'tp'=8] {'chip'}, dimensions={0} | all-to-all | bytes 2097152 | tf_op jit(solution)/shard_map/all_to_all | solution.py:400
  75.5 1.1 %shard_map.100 = (bf16[256,1024]{1,0:T(8,128)(2,1)}, bf16[256,1024]{1,0:T(8,128)(2,1)}) custom-call(bf16[8,2,256,128]{3,2,1,0:T(8,128)(2,1)S(1)} %bitcast.20), custom_call_target="tpu_custom_call" | custom-call | bytes 2097152 | tf_op jit(solution)/shard_map/pallas_call | solution.py:141
  (1 shorter events, 0.0 us)
Async XLA Ops:
  0.6 35.5 %copy-start = (f32[1024]{0:T(1024)S(1)}, f32[1024]{0:T(1024)}, u32[]{:S(2)}) copy-start(f32[1024]{0:T(1024)} %param.11) | copy-start | bytes 12292
  3.0 6.1 %copy-start.2 = (bf16[256,1024]{1,0:T(8,128)(2,1)S(1)}, bf16[256,1024]{1,0:T(8,128)(2,1)}, u32[]{:S(2)}) copy-start(bf16[256,1024]{1,0:T(8,128)(2,1)} %queries.1) | copy-start | bytes 1572868
  3.0 6.1 %copy-start.3 = (bf16[256,1024]{1,0:T(8,128)(2,1)S(1)}, bf16[256,1024]{1,0:T(8,128)(2,1)}, u32[]{:S(2)}) copy-start(bf16[256,1024]{1,0:T(8,128)(2,1)} %keys.1) | copy-start | bytes 1572868
  3.0 6.1 %copy-start.6 = (bf16[512,256]{1,0:T(8,128)(2,1)S(1)}, bf16[512,256]{1,0:T(8,128)(2,1)}, u32[]{:S(2)}) copy-start(bf16[512,256]{1,0:T(8,128)(2,1)} %constant.21.clone.forward) | copy-start | bytes 786436
  3.1 26.5 %all-to-all-start = ((bf16[8,768,128]{2,1,0:T(8,128)(2,1)}), bf16[8,768,128]{2,1,0:T(8,128)(2,1)S(1)}, u32[]{:S(2)}, u32[]{:S(2)}) async-start(bf16[8,768,128]{2,1,0:T(8,128)(2,1)} %bitcast.1), calls=%async_computation | async-start | bytes 3145728 | tf_op jit(solution)/shard_map/all_to_all | solution.py:400
  9.4 1.0 %copy-start.1 = (bf16[8,2,256,128]{3,2,1,0:T(8,128)(2,1)}, bf16[8,2,256,128]{3,2,1,0:T(8,128)(2,1)S(1)}, u32[]{:S(2)}) copy-start(bf16[8,2,256,128]{3,2,1,0:T(8,128)(2,1)S(1)} %get-tuple-element.16) | copy-start | bytes 3145732
  29.6 18.1 %all-to-all-start.1 = ((bf16[8,512,128]{2,1,0:T(8,128)(2,1)}), bf16[8,512,128]{2,1,0:T(8,128)(2,1)S(1)}, u32[]{:S(2)}, u32[]{:S(2)}) async-start(bf16[8,512,128]{2,1,0:T(8,128)(2,1)} %bitcast.22), calls=%async_computation.1 | async-start | bytes 2097152 | tf_op jit(solution)/shard_map/all_to_all | solution.py:400
  34.4 3.9 %collective-permute-start.1 = (bf16[8,256,128]{2,1,0:T(8,128)(2,1)}, bf16[8,256,128]{2,1,0:T(8,128)(2,1)}, u32[]{:S(2)}, u32[]{:S(2)}) collective-permute-start(bf16[8,256,128]{2,1,0:T(8,128)(2,1)} %get-tuple-element.26), channel_id=1, source_target_pairs={{0,8},{8,0},{1,9},{9,1},{2,10},{10,2},{3,11},{11,3},{4,12},{12,4},... | collective-permute-start | bytes 1572872 | tf_op jit(solution)/shard_map/ppermute | solution.py:405
  36.1 2.5 %collective-permute-start = (bf16[8,256,128]{2,1,0:T(8,128)(2,1)}, bf16[8,256,128]{2,1,0:T(8,128)(2,1)S(1)}, u32[]{:S(2)}, u32[]{:S(2)}) collective-permute-start(bf16[8,256,128]{2,1,0:T(8,128)(2,1)} %get-tuple-element.27), channel_id=1, source_target_pairs={{0,8},{8,0},{1,9},{9,1},{2,10},{10,2},{3,11},{11,3},{4,12},{12,4},... | collective-permute-start | bytes 1572872 | tf_op jit(solution)/shard_map/ppermute | solution.py:405
  45.7 1.6 %copy-start.4 = (bf16[4,256,128]{2,1,0:T(8,128)(2,1)}, bf16[4,256,128]{2,1,0:T(8,128)(2,1)S(1)}, u32[]{:S(2)}) copy-start(bf16[4,256,128]{2,1,0:T(8,128)(2,1)S(1)} %get-tuple-element.19.refs_0_) | copy-start | bytes 786436
  45.7 1.6 %copy-start.5 = (bf16[4,256,128]{2,1,0:T(8,128)(2,1)}, bf16[4,256,128]{2,1,0:T(8,128)(2,1)S(1)}, u32[]{:S(2)}) copy-start(bf16[4,256,128]{2,1,0:T(8,128)(2,1)S(1)} %get-tuple-element.20.refs_1_) | copy-start | bytes 786436
  45.7 1.6 %collective-permute-start.2 = (bf16[4,256,128]{2,1,0:T(8,128)(2,1)S(1)}, bf16[4,256,128]{2,1,0:T(8,128)(2,1)S(1)}, u32[]{:S(2)}, u32[]{:S(2)}) collective-permute-start(bf16[4,256,128]{2,1,0:T(8,128)(2,1)S(1)} %get-tuple-element.19.refs_0_), channel_id=1, source_target_pairs={{0,8},{8,0},{1,9},{9,1},{2,10},{10,2},{3,11},{11,3},{4,12},{12,4},... | collective-permute-start | bytes 786440 | tf_op jit(solution)/shard_map/ppermute | solution.py:405
  46.2 1.5 %collective-permute-start.3 = (bf16[4,256,128]{2,1,0:T(8,128)(2,1)S(1)}, bf16[4,256,128]{2,1,0:T(8,128)(2,1)S(1)}, u32[]{:S(2)}, u32[]{:S(2)}) collective-permute-start(bf16[4,256,128]{2,1,0:T(8,128)(2,1)S(1)} %get-tuple-element.20.refs_1_), channel_id=1, source_target_pairs={{0,8},{8,0},{1,9},{9,1},{2,10},{10,2},{3,11},{11,3},{4,12},{12,4},... | collective-permute-start | bytes 786440 | tf_op jit(solution)/shard_map/ppermute | solution.py:405
  47.8 5.9 %collective-permute-start.4 = (bf16[8,256,128]{2,1,0:T(8,128)(2,1)S(1)}, bf16[8,256,128]{2,1,0:T(8,128)(2,1)S(1)}, u32[]{:S(2)}, u32[]{:S(2)}) collective-permute-start(bf16[8,256,128]{2,1,0:T(8,128)(2,1)S(1)} %slice_bitcast_fusion), channel_id=1, source_target_pairs={{0,8},{8,0},{1,9},{9,1},{2,10},{10,2},{3,11},{11,3},{4,12},{12,4},... | collective-permute-start | bytes 1572872 | tf_op jit(solution)/shard_map/ppermute | solution.py:405

commit v5 on v4

--- a/solution.py
+++ b/solution.py
@@ -378,7 +378,7 @@
         out[b, 1] = (total[:, :lanes] / total[:, lanes:]).astype(jnp.bfloat16)
 
     values = [v_other[j // each].at[j % each] for j in range(blocks)]
-    sweep(blocks, make_scores, values, begin, finish)
+    sweep(blocks, make_scores, values, begin, finish, 1)
     for c in stores:
         c.wait()
 

time: 76.9 us -> 76.8 us (level)
  no operation moved by 1% of the time
where the time goes in v5:
time: 76.8 us; the launch traced here: 76.5 us
  waiting for transfers between devices  23 us (30%)
  blocking collectives  18.6 us (24%)
  Pallas kernels  17.4 us (23%)
  starting transfers between devices  14.5 us (19%)
  local copies, waits for them, and re-layouts  2.17 us (3%)
  between operations  0.77 us (1%)
    all_to_all x2, waiting for transfers between devices, to_chips(): lax.all_to_all(flat, 'chip', split_axis=0, concat_axis=0, tiled=True)  19.2 us
    all_to_all x1, blocking collectives, to_chips(): lax.all_to_all(flat, 'chip', split_axis=0, concat_axis=0, tiled=True)  18.6 us
    all_to_all x2, starting transfers between devices, to_chips(): lax.all_to_all(flat, 'chip', split_axis=0, concat_axis=0, tiled=True)  9.87 us
    pallas_call x1, Pallas kernels, convolve(): pl.pallas_call(conv_kernel, in_specs=[SMEM, VMEM, VMEM, ANYWHERE, VMEM, V...  7.13 us
    ppermute x5, starting transfers between devices, swap(): return lax.ppermute(array, 'core', [(0, 1), (1, 0)])  4.63 us
    ppermute x5, waiting for transfers between devices, swap(): return lax.ppermute(array, 'core', [(0, 1), (1, 0)])  3.81 us
    pallas_call x1, Pallas kernels, attend_own(): pl.pallas_call(own_kernel, in_specs=[VMEM] + [ANYWHERE] * PARTS, out_spec...  3.51 us
    pallas_call x1, Pallas kernels, attend_other(): pl.pallas_call(other_kernel, in_specs=[SMEM] + [VMEM] * 4 + [ANYWHERE] *...  3.14 us
  transfers between devices with their start and end apart: 7, of which 5 were waited for; matrix products, arithmetic and copies ran while one was open for 1% of the time, Pallas kernels for 14%

profile of v5, /device:TPU:1, one launch (start us, length us, event | category | flops | bytes accessed | tf_op | source)
XLA Modules:
  0.0 76.5 jit_solution(3822670562275212375)
XLA Ops:
  0.6 0.0 copy-start
  0.6 2.4 %shard_map.95 = bf16[8,3,256,128]{3,2,1,0:T(8,128)(2,1)} custom-call(bf16[256,1024]{1,0:T(8,128)(2,1)} %refs_0_.1, f32[256,1024]{1,0:T(8,128)} %refs_1_.1, bf16[256,1024]{1,0:T(8,128)(2,1)} %refs_2_.1), custom_call_target="tpu_custom_call" | custom-call | bytes 6291456 | tf_op jit(solution)/shard_map/pallas_call | solution.py:91
  3.0 0.0 copy-start.2
  3.0 0.0 copy-start.3
  3.0 0.0 copy-start.6
  3.1 6.1 %all-to-all-start = ((bf16[8,768,128]{2,1,0:T(8,128)(2,1)}), bf16[8,768,128]{2,1,0:T(8,128)(2,1)S(1)}, u32[]{:S(2)}, u32[]{:S(2)}) async-start(bf16[8,768,128]{2,1,0:T(8,128)(2,1)} %bitcast.1), calls=%async_computation | async-start | bytes 3145728 | tf_op jit(solution)/shard_map/all_to_all | solution.py:400
  9.2 0.0 copy-done.2
  9.2 0.0 copy-done.3
  9.2 0.0 copy-done.6
  9.2 0.2 shard_map.96
  9.4 0.0 copy-start.1
  9.4 1.0 %copy-done.1 = bf16[8,2,256,128]{3,2,1,0:T(8,128)(2,1)} copy-done((bf16[8,2,256,128]{3,2,1,0:T(8,128)(2,1)}, bf16[8,2,256,128]{3,2,1,0:T(8,128)(2,1)S(1)}, u32[]{:S(2)}) %copy-start.1) | copy-done | bytes 1048600
  10.4 19.2 %all-to-all-done = bf16[8,768,128]{2,1,0:T(8,128)(2,1)S(1)} async-done(((bf16[8,768,128]{2,1,0:T(8,128)(2,1)}), bf16[8,768,128]{2,1,0:T(8,128)(2,1)S(1)}, u32[]{:S(2)}, u32[]{:S(2)}) %all-to-all-start) | async-done | bytes 1572896 | tf_op jit(solution)/shard_map/all_to_all | solution.py:400
  29.6 3.8 %all-to-all-start.1 = ((bf16[8,512,128]{2,1,0:T(8,128)(2,1)}), bf16[8,512,128]{2,1,0:T(8,128)(2,1)S(1)}, u32[]{:S(2)}, u32[]{:S(2)}) async-start(bf16[8,512,128]{2,1,0:T(8,128)(2,1)} %bitcast.22), calls=%async_computation.1 | async-start | bytes 2097152 | tf_op jit(solution)/shard_map/all_to_all | solution.py:400
  33.4 1.0 %slice_bitcast_fusion.1 = (bf16[8,256,128]{2,1,0:T(8,128)(2,1)}, bf16[8,256,128]{2,1,0:T(8,128)(2,1)}) fusion(bf16[8,3,256,128]{3,2,1,0:T(8,128)(2,1)S(1)} %bitcast.15), kind=kLoop, calls=%fused_computation.1 | loop fusion | bytes 2097152 | tf_op jit(solution)/shard_map/squeeze | solution.py:416
  34.4 1.6 %collective-permute-start.1 = (bf16[8,256,128]{2,1,0:T(8,128)(2,1)}, bf16[8,256,128]{2,1,0:T(8,128)(2,1)}, u32[]{:S(2)}, u32[]{:S(2)}) collective-permute-start(bf16[8,256,128]{2,1,0:T(8,128)(2,1)} %get-tuple-element.26), channel_id=1, source_target_pairs={{0,8},{8,0},{1,9},{9,1},{2,10},{10,2},{3,11},{11,3},{4,12},{12,4},... | collective-permute-start | bytes 1572872 | tf_op jit(solution)/shard_map/ppermute | solution.py:405
  36.1 0.0 collective-permute-start
  36.1 0.0 copy-done
  36.1 0.1 dynamic-slice_bitcast_fusion.skip_ref
  36.2 2.2 %collective-permute-done.1.h_any = bf16[8,256,128]{2,1,0:T(8,128)(2,1)} collective-permute-done((bf16[8,256,128]{2,1,0:T(8,128)(2,1)}, bf16[8,256,128]{2,1,0:T(8,128)(2,1)}, u32[]{:S(2)}, u32[]{:S(2)}) %collective-permute-start.1) | collective-permute-done | bytes 524320 | tf_op jit(solution)/shard_map/ppermute | solution.py:405
  38.3 0.2 collective-permute-done.x_other
  38.6 7.1 %shard_map.97 = (bf16[4,256,128]{2,1,0:T(8,128)(2,1)S(1)}, bf16[4,256,128]{2,1,0:T(8,128)(2,1)S(1)}) custom-call(s32[1]{0:T(128)} %bitcast.core_ref, bf16[8,3,256,128]{3,2,1,0:T(8,128)(2,1)S(1)} %bitcast.16, bf16[8,256,128]{2,1,0:T(8,128)(2,1)S(1)} %collective-permute-done.x_other, bf16[8,256,128]{2,1,0:T(8,128)(2,1)} %collective-permute-done.1.h_any, ...), custom_call_target="tpu_custom_call" | custom-call | flops 1000000 | bytes 1048576 | tf_op jit(solution)/shard_map/pallas_call | solution.py:233
  45.7 0.0 copy-start.4
  45.7 0.0 copy-start.5
  45.7 0.5 collective-permute-start.2
  46.2 0.1 collective-permute-start.3
  46.3 1.0 %collective-permute-done.2.refs_2_ = bf16[4,256,128]{2,1,0:T(8,128)(2,1)S(1)} collective-permute-done((bf16[4,256,128]{2,1,0:T(8,128)(2,1)S(1)}, bf16[4,256,128]{2,1,0:T(8,128)(2,1)S(1)}, u32[]{:S(2)}, u32[]{:S(2)}) %collective-permute-start.2) | collective-permute-done | bytes 262176 | tf_op jit(solution)/shard_map/ppermute | solution.py:405
  47.4 0.0 copy-done.4
  47.4 0.0 copy-done.5
  47.4 0.4 collective-permute-done.3.refs_3_
  47.7 0.0 all-to-all-done.1
  47.8 2.4 %collective-permute-start.4 = (bf16[8,256,128]{2,1,0:T(8,128)(2,1)S(1)}, bf16[8,256,128]{2,1,0:T(8,128)(2,1)S(1)}, u32[]{:S(2)}, u32[]{:S(2)}) collective-permute-start(bf16[8,256,128]{2,1,0:T(8,128)(2,1)S(1)} %slice_bitcast_fusion), channel_id=1, source_target_pairs={{0,8},{8,0},{1,9},{9,1},{2,10},{10,2},{3,11},{11,3},{4,12},{12,4},... | collective-permute-start | bytes 1572872 | tf_op jit(solution)/shard_map/ppermute | solution.py:405
  50.2 3.5 %shard_map.98 = (f32[8,256,256]{2,1,0:T(8,128)S(1)}, f32[8,256,128]{2,1,0:T(8,128)S(1)}) custom-call(bf16[8,2,256,128]{3,2,1,0:T(8,128)(2,1)S(1)} %bitcast.18, bf16[4,256,128]{2,1,0:T(8,128)(2,1)} %copy-done.4, bf16[4,256,128]{2,1,0:T(8,128)(2,1)} %copy-done.5), custom_call_target="tpu_custom_call" | custom-call | flops 1000000000 | bytes 1048576 | tf_op jit(solution)/shard_map/pallas_call | solution.py:335
  53.7 0.0 collective-permute-done.4.k_other
  53.7 3.1 %shard_map.99 = bf16[8,2,256,128]{3,2,1,0:T(8,128)(2,1)S(1)} custom-call(s32[1]{0:T(128)} %bitcast.core_ref, bf16[8,2,256,128]{3,2,1,0:T(8,128)(2,1)S(1)} %bitcast.19, bf16[8,256,128]{2,1,0:T(8,128)(2,1)S(1)} %collective-permute-done.4.k_other, f32[8,256,256]{2,1,0:T(8,128)S(1)} %get-tuple-element.22.total_ref, ...), custom_call_target="tpu_custom_call" | custom-call | flops 1000000000 | bytes 1048576 | tf_op jit(solution)/shard_map/pallas_call | solution.py:388
  56.8 18.6 %all_to_all.15 = bf16[8,512,128]{2,1,0:T(8,128)(2,1)S(1)} all-to-all(bf16[8,512,128]{2,1,0:T(8,128)(2,1)S(1)} %bitcast.21), channel_id=1, replica_groups=mesh['chip'=8,'core'=2,'tp'=8] {'chip'}, dimensions={0} | all-to-all | bytes 2097152 | tf_op jit(solution)/shard_map/all_to_all | solution.py:400
  75.4 1.1 %shard_map.100 = (bf16[256,1024]{1,0:T(8,128)(2,1)}, bf16[256,1024]{1,0:T(8,128)(2,1)}) custom-call(bf16[8,2,256,128]{3,2,1,0:T(8,128)(2,1)S(1)} %bitcast.20), custom_call_target="tpu_custom_call" | custom-call | bytes 2097152 | tf_op jit(solution)/shard_map/pallas_call | solution.py:141
  (1 shorter events, 0.0 us)
Async XLA Ops:
  0.6 35.5 %copy-start = (f32[1024]{0:T(1024)S(1)}, f32[1024]{0:T(1024)}, u32[]{:S(2)}) copy-start(f32[1024]{0:T(1024)} %param.11) | copy-start | bytes 12292
  3.0 6.1 %copy-start.2 = (bf16[256,1024]{1,0:T(8,128)(2,1)S(1)}, bf16[256,1024]{1,0:T(8,128)(2,1)}, u32[]{:S(2)}) copy-start(bf16[256,1024]{1,0:T(8,128)(2,1)} %queries.1) | copy-start | bytes 1572868
  3.0 6.1 %copy-start.3 = (bf16[256,1024]{1,0:T(8,128)(2,1)S(1)}, bf16[256,1024]{1,0:T(8,128)(2,1)}, u32[]{:S(2)}) copy-start(bf16[256,1024]{1,0:T(8,128)(2,1)} %keys.1) | copy-start | bytes 1572868
  3.0 6.1 %copy-start.6 = (bf16[512,256]{1,0:T(8,128)(2,1)S(1)}, bf16[512,256]{1,0:T(8,128)(2,1)}, u32[]{:S(2)}) copy-start(bf16[512,256]{1,0:T(8,128)(2,1)} %constant.21.clone.forward) | copy-start | bytes 786436
  3.1 26.5 %all-to-all-start = ((bf16[8,768,128]{2,1,0:T(8,128)(2,1)}), bf16[8,768,128]{2,1,0:T(8,128)(2,1)S(1)}, u32[]{:S(2)}, u32[]{:S(2)}) async-start(bf16[8,768,128]{2,1,0:T(8,128)(2,1)} %bitcast.1), calls=%async_computation | async-start | bytes 3145728 | tf_op jit(solution)/shard_map/all_to_all | solution.py:400
  9.4 1.0 %copy-start.1 = (bf16[8,2,256,128]{3,2,1,0:T(8,128)(2,1)}, bf16[8,2,256,128]{3,2,1,0:T(8,128)(2,1)S(1)}, u32[]{:S(2)}) copy-start(bf16[8,2,256,128]{3,2,1,0:T(8,128)(2,1)S(1)} %get-tuple-element.16) | copy-start | bytes 3145732
  29.6 18.1 %all-to-all-start.1 = ((bf16[8,512,128]{2,1,0:T(8,128)(2,1)}), bf16[8,512,128]{2,1,0:T(8,128)(2,1)S(1)}, u32[]{:S(2)}, u32[]{:S(2)}) async-start(bf16[8,512,128]{2,1,0:T(8,128)(2,1)} %bitcast.22), calls=%async_computation.1 | async-start | bytes 2097152 | tf_op jit(solution)/shard_map/all_to_all | solution.py:400
  34.4 3.9 %collective-permute-start.1 = (bf16[8,256,128]{2,1,0:T(8,128)(2,1)}, bf16[8,256,128]{2,1,0:T(8,128)(2,1)}, u32[]{:S(2)}, u32[]{:S(2)}) collective-permute-start(bf16[8,256,128]{2,1,0:T(8,128)(2,1)} %get-tuple-element.26), channel_id=1, source_target_pairs={{0,8},{8,0},{1,9},{9,1},{2,10},{10,2},{3,11},{11,3},{4,12},{12,4},... | collective-permute-start | bytes 1572872 | tf_op jit(solution)/shard_map/ppermute | solution.py:405
  36.1 2.5 %collective-permute-start = (bf16[8,256,128]{2,1,0:T(8,128)(2,1)}, bf16[8,256,128]{2,1,0:T(8,128)(2,1)S(1)}, u32[]{:S(2)}, u32[]{:S(2)}) collective-permute-start(bf16[8,256,128]{2,1,0:T(8,128)(2,1)} %get-tuple-element.27), channel_id=1, source_target_pairs={{0,8},{8,0},{1,9},{9,1},{2,10},{10,2},{3,11},{11,3},{4,12},{12,4},... | collective-permute-start | bytes 1572872 | tf_op jit(solution)/shard_map/ppermute | solution.py:405
  45.7 1.6 %copy-start.4 = (bf16[4,256,128]{2,1,0:T(8,128)(2,1)}, bf16[4,256,128]{2,1,0:T(8,128)(2,1)S(1)}, u32[]{:S(2)}) copy-start(bf16[4,256,128]{2,1,0:T(8,128)(2,1)S(1)} %get-tuple-element.19.refs_0_) | copy-start | bytes 786436
  45.7 1.6 %copy-start.5 = (bf16[4,256,128]{2,1,0:T(8,128)(2,1)}, bf16[4,256,128]{2,1,0:T(8,128)(2,1)S(1)}, u32[]{:S(2)}) copy-start(bf16[4,256,128]{2,1,0:T(8,128)(2,1)S(1)} %get-tuple-element.20.refs_1_) | copy-start | bytes 786436
  45.7 1.6 %collective-permute-start.2 = (bf16[4,256,128]{2,1,0:T(8,128)(2,1)S(1)}, bf16[4,256,128]{2,1,0:T(8,128)(2,1)S(1)}, u32[]{:S(2)}, u32[]{:S(2)}) collective-permute-start(bf16[4,256,128]{2,1,0:T(8,128)(2,1)S(1)} %get-tuple-element.19.refs_0_), channel_id=1, source_target_pairs={{0,8},{8,0},{1,9},{9,1},{2,10},{10,2},{3,11},{11,3},{4,12},{12,4},... | collective-permute-start | bytes 786440 | tf_op jit(solution)/shard_map/ppermute | solution.py:405
  46.2 1.5 %collective-permute-start.3 = (bf16[4,256,128]{2,1,0:T(8,128)(2,1)S(1)}, bf16[4,256,128]{2,1,0:T(8,128)(2,1)S(1)}, u32[]{:S(2)}, u32[]{:S(2)}) collective-permute-start(bf16[4,256,128]{2,1,0:T(8,128)(2,1)S(1)} %get-tuple-element.20.refs_1_), channel_id=1, source_target_pairs={{0,8},{8,0},{1,9},{9,1},{2,10},{10,2},{3,11},{11,3},{4,12},{12,4},... | collective-permute-start | bytes 786440 | tf_op jit(solution)/shard_map/ppermute | solution.py:405
  47.8 5.9 %collective-permute-start.4 = (bf16[8,256,128]{2,1,0:T(8,128)(2,1)S(1)}, bf16[8,256,128]{2,1,0:T(8,128)(2,1)S(1)}, u32[]{:S(2)}, u32[]{:S(2)}) collective-permute-start(bf16[8,256,128]{2,1,0:T(8,128)(2,1)S(1)} %slice_bitcast_fusion), channel_id=1, source_target_pairs={{0,8},{8,0},{1,9},{9,1},{2,10},{10,2},{3,11},{11,3},{4,12},{12,4},... | collective-permute-start | bytes 1572872 | tf_op jit(solution)/shard_map/ppermute | solution.py:405

commit v6 on v5

--- a/solution.py
+++ b/solution.py
@@ -14,7 +14,7 @@
 CORES = 2
 SCALE = 1.0 / math.sqrt(HEAD_DIM)
 MASKED = -1e30
-PARTS = 2
+PARTS = 1
 TO_EXP2 = SCALE * math.log2(math.e)
 MIB = 1024 * 1024
 

time: 76.8 us -> 79.1 us (1.030)
  waiting for transfers between devices: 23 us -> 24.9 us
  local copies, waits for them, and re-layouts: 2.17 us -> 4.01 us
  starting transfers between devices: 14.5 us -> 13.5 us
    all_to_all x2, waiting for transfers between devices: 19.2 us -> 24.9 us  [to_chips(): lax.all_to_all(flat, 'chip', split_axis=0, concat_axis=0, tiled=True)]
    ppermute x5 -> x4, waiting for transfers between devices: 3.81 us -> 0.01 us  [swap(): return lax.ppermute(array, 'core', [(0, 1), (1, 0)])]
    unnamed x14 -> x16, local copies, waits for them, and re-layouts: 1.02 us -> 2.86 us
    ppermute x5 -> x4, starting transfers between devices: 4.63 us -> 3.89 us  [swap(): return lax.ppermute(array, 'core', [(0, 1), (1, 0)])]
  transfers between devices with their start and end apart: 7 -> 6, of which waited for: 5 -> 2; matrix products, arithmetic and copies ran while one was open for 1% -> 0% of each run, Pallas kernels for 14% -> 14%
where the time goes in v6:
time: 79.1 us; the launch traced here: 78.7 us
  waiting for transfers between devices  24.9 us (31%)
  blocking collectives  18 us (23%)
  Pallas kernels  17.4 us (22%)
  starting transfers between devices  13.5 us (17%)
  local copies, waits for them, and re-layouts  4.01 us (5%)
    all_to_all x2, waiting for transfers between devices, to_chips(): lax.all_to_all(flat, 'chip', split_axis=0, concat_axis=0, tiled=True)  24.9 us
    all_to_all x1, blocking collectives, to_chips(): lax.all_to_all(flat, 'chip', split_axis=0, concat_axis=0, tiled=True)  18 us
    all_to_all x2, starting transfers between devices, to_chips(): lax.all_to_all(flat, 'chip', split_axis=0, concat_axis=0, tiled=True)  9.65 us
    pallas_call x1, Pallas kernels, convolve(): pl.pallas_call(conv_kernel, in_specs=[SMEM, VMEM, VMEM, ANYWHERE, VMEM, V...  7.02 us
    ppermute x4, starting transfers between devices, swap(): return lax.ppermute(array, 'core', [(0, 1), (1, 0)])  3.89 us
    pallas_call x1, Pallas kernels, attend_own(): pl.pallas_call(own_kernel, in_specs=[VMEM] + [ANYWHERE] * PARTS, out_spec...  3.51 us
    pallas_call x1, Pallas kernels, attend_other(): pl.pallas_call(other_kernel, in_specs=[SMEM] + [VMEM] * 4 + [ANYWHERE] *...  3.12 us
    unnamed x16, local copies, waits for them, and re-layouts  2.86 us
  transfers between devices with their start and end apart: 6, of which 2 were waited for; matrix products, arithmetic and copies ran while one was open for 0% of the time, Pallas kernels for 14%

profile of v6, /device:TPU:1, one launch (start us, length us, event | category | flops | bytes accessed | tf_op | source)
XLA Modules:
  0.0 78.7 jit_solution(9458365002455288117)
XLA Ops:
  0.6 0.0 copy-start
  0.6 2.4 %shard_map.95 = bf16[8,3,256,128]{3,2,1,0:T(8,128)(2,1)} custom-call(bf16[256,1024]{1,0:T(8,128)(2,1)} %refs_0_.1, f32[256,1024]{1,0:T(8,128)} %refs_1_.1, bf16[256,1024]{1,0:T(8,128)(2,1)} %refs_2_.1), custom_call_target="tpu_custom_call" | custom-call | bytes 6291456 | tf_op jit(solution)/shard_map/pallas_call | solution.py:91
  3.1 0.0 copy-start.3
  3.1 0.0 copy-start.4
  3.1 0.0 copy-start.7
  3.1 6.1 %all-to-all-start = ((bf16[8,768,128]{2,1,0:T(8,128)(2,1)}), bf16[8,768,128]{2,1,0:T(8,128)(2,1)S(1)}, u32[]{:S(2)}, u32[]{:S(2)}) async-start(bf16[8,768,128]{2,1,0:T(8,128)(2,1)} %bitcast.1), calls=%async_computation | async-start | bytes 3145728 | tf_op jit(solution)/shard_map/all_to_all | solution.py:400
  9.2 0.0 copy-done.3
  9.2 0.0 copy-done.4
  9.2 0.0 copy-done.7
  9.3 0.2 shard_map.96
  9.5 0.0 copy-start.2
  9.5 1.0 %copy-done.2 = bf16[8,2,256,128]{3,2,1,0:T(8,128)(2,1)} copy-done((bf16[8,2,256,128]{3,2,1,0:T(8,128)(2,1)}, bf16[8,2,256,128]{3,2,1,0:T(8,128)(2,1)S(1)}, u32[]{:S(2)}) %copy-start.2) | copy-done | bytes 1048600
  10.5 19.2 %all-to-all-done = bf16[8,768,128]{2,1,0:T(8,128)(2,1)S(1)} async-done(((bf16[8,768,128]{2,1,0:T(8,128)(2,1)}), bf16[8,768,128]{2,1,0:T(8,128)(2,1)S(1)}, u32[]{:S(2)}, u32[]{:S(2)}) %all-to-all-start) | async-done | bytes 1572896 | tf_op jit(solution)/shard_map/all_to_all | solution.py:400
  29.7 1.0 %slice_bitcast_fusion.1 = (bf16[8,256,128]{2,1,0:T(8,128)(2,1)}, bf16[8,256,128]{2,1,0:T(8,128)(2,1)}) fusion(bf16[8,3,256,128]{3,2,1,0:T(8,128)(2,1)S(1)} %bitcast.15), kind=kLoop, calls=%fused_computation.1 | loop fusion | bytes 2097152 | tf_op jit(solution)/shard_map/squeeze | solution.py:416
  30.7 1.9 %collective-permute-start.1 = (bf16[8,256,128]{2,1,0:T(8,128)(2,1)}, bf16[8,256,128]{2,1,0:T(8,128)(2,1)}, u32[]{:S(2)}, u32[]{:S(2)}) collective-permute-start(bf16[8,256,128]{2,1,0:T(8,128)(2,1)} %get-tuple-element.20), channel_id=1, source_target_pairs={{0,8},{8,0},{1,9},{9,1},{2,10},{10,2},{3,11},{11,3},{4,12},{12,4},... | collective-permute-start | bytes 1572872 | tf_op jit(solution)/shard_map/ppermute | solution.py:405
  32.6 0.0 collective-permute-start
  32.6 3.6 %all-to-all-start.1 = ((bf16[8,512,128]{2,1,0:T(8,128)(2,1)}), bf16[8,512,128]{2,1,0:T(8,128)(2,1)S(1)}, u32[]{:S(2)}, u32[]{:S(2)}) async-start(bf16[8,512,128]{2,1,0:T(8,128)(2,1)} %bitcast.22), calls=%async_computation.1 | async-start | bytes 2097152 | tf_op jit(solution)/shard_map/all_to_all | solution.py:400
  36.2 0.0 copy-done
  36.2 0.1 dynamic-slice_bitcast_fusion.skip_ref
  36.2 0.0 collective-permute-done.1.h_any
  36.3 0.0 collective-permute-done.x_other
  36.3 0.0 copy-start.5
  36.3 0.8 %copy-done.5 = bf16[8,256,128]{2,1,0:T(8,128)(2,1)} copy-done((bf16[8,256,128]{2,1,0:T(8,128)(2,1)}, bf16[8,256,128]{2,1,0:T(8,128)(2,1)S(1)}, u32[]{:S(2)}) %copy-start.5) | copy-done | bytes 524312
  37.1 0.0 copy-start.6
  37.1 1.0 %copy-done.6 = bf16[8,256,128]{2,1,0:T(8,128)(2,1)S(1)} copy-done((bf16[8,256,128]{2,1,0:T(8,128)(2,1)S(1)}, bf16[8,256,128]{2,1,0:T(8,128)(2,1)}, u32[]{:S(2)}) %copy-start.6) | copy-done | bytes 524312
  38.1 7.0 %shard_map.97.refs_0_ = bf16[8,256,128]{2,1,0:T(8,128)(2,1)S(1)} custom-call(s32[1]{0:T(128)} %bitcast.core_ref, bf16[8,3,256,128]{3,2,1,0:T(8,128)(2,1)S(1)} %bitcast.16, bf16[8,256,128]{2,1,0:T(8,128)(2,1)S(1)} %copy-done.6, bf16[8,256,128]{2,1,0:T(8,128)(2,1)} %collective-permute-done.1.h_any, f32[1,128]{1,0:T(1,128)S(1)} %dynamic-slice_bitcast_fusion.skip_ref, ...), custom_call_target="tpu_custom_call" | custom-call | flops 1000000 | bytes 1048576 | tf_op jit(solution)/shard_map/pallas_call | solution.py:233
  45.1 0.0 copy-start.1
  45.1 0.6 collective-permute-start.2
  45.7 5.7 %all-to-all-done.1 = bf16[8,512,128]{2,1,0:T(8,128)(2,1)S(1)} async-done(((bf16[8,512,128]{2,1,0:T(8,128)(2,1)}), bf16[8,512,128]{2,1,0:T(8,128)(2,1)S(1)}, u32[]{:S(2)}, u32[]{:S(2)}) %all-to-all-start.1) | async-done | bytes 1048608 | tf_op jit(solution)/shard_map/all_to_all | solution.py:400
  51.4 0.0 collective-permute-done.2.refs_1_
  51.5 1.4 %collective-permute-start.3 = (bf16[8,256,128]{2,1,0:T(8,128)(2,1)S(1)}, bf16[8,256,128]{2,1,0:T(8,128)(2,1)S(1)}, u32[]{:S(2)}, u32[]{:S(2)}) collective-permute-start(bf16[8,256,128]{2,1,0:T(8,128)(2,1)S(1)} %slice_bitcast_fusion), channel_id=1, source_target_pairs={{0,8},{8,0},{1,9},{9,1},{2,10},{10,2},{3,11},{11,3},{4,12},{12,4},... | collective-permute-start | bytes 1572872 | tf_op jit(solution)/shard_map/ppermute | solution.py:405
  52.9 0.0 copy-done.1
  52.9 3.5 %shard_map.98 = (f32[8,256,256]{2,1,0:T(8,128)S(1)}, f32[8,256,128]{2,1,0:T(8,128)S(1)}) custom-call(bf16[8,2,256,128]{3,2,1,0:T(8,128)(2,1)S(1)} %bitcast.18, bf16[8,256,128]{2,1,0:T(8,128)(2,1)} %copy-done.1), custom_call_target="tpu_custom_call" | custom-call | flops 1000000000 | bytes 1048576 | tf_op jit(solution)/shard_map/pallas_call | solution.py:335
  56.4 0.0 collective-permute-done.3.k_other
  56.4 3.1 %shard_map.99 = bf16[8,2,256,128]{3,2,1,0:T(8,128)(2,1)S(1)} custom-call(s32[1]{0:T(128)} %bitcast.core_ref, bf16[8,2,256,128]{3,2,1,0:T(8,128)(2,1)S(1)} %bitcast.19, bf16[8,256,128]{2,1,0:T(8,128)(2,1)S(1)} %collective-permute-done.3.k_other, f32[8,256,256]{2,1,0:T(8,128)S(1)} %get-tuple-element.17.total_ref, ...), custom_call_target="tpu_custom_call" | custom-call | flops 1000000000 | bytes 1048576 | tf_op jit(solution)/shard_map/pallas_call | solution.py:388
  59.6 18.0 %all_to_all.15 = bf16[8,512,128]{2,1,0:T(8,128)(2,1)S(1)} all-to-all(bf16[8,512,128]{2,1,0:T(8,128)(2,1)S(1)} %bitcast.21), channel_id=1, replica_groups=mesh['chip'=8,'core'=2,'tp'=8] {'chip'}, dimensions={0} | all-to-all | bytes 2097152 | tf_op jit(solution)/shard_map/all_to_all | solution.py:400
  77.6 1.1 %shard_map.100 = (bf16[256,1024]{1,0:T(8,128)(2,1)}, bf16[256,1024]{1,0:T(8,128)(2,1)}) custom-call(bf16[8,2,256,128]{3,2,1,0:T(8,128)(2,1)S(1)} %bitcast.20), custom_call_target="tpu_custom_call" | custom-call | bytes 2097152 | tf_op jit(solution)/shard_map/pallas_call | solution.py:141
  (1 shorter events, 0.0 us)
Async XLA Ops:
  0.6 35.5 %copy-start = (f32[1024]{0:T(1024)S(1)}, f32[1024]{0:T(1024)}, u32[]{:S(2)}) copy-start(f32[1024]{0:T(1024)} %param.11) | copy-start | bytes 12292
  3.1 6.1 %copy-start.3 = (bf16[256,1024]{1,0:T(8,128)(2,1)S(1)}, bf16[256,1024]{1,0:T(8,128)(2,1)}, u32[]{:S(2)}) copy-start(bf16[256,1024]{1,0:T(8,128)(2,1)} %queries.1) | copy-start | bytes 1572868
  3.1 6.1 %copy-start.4 = (bf16[256,1024]{1,0:T(8,128)(2,1)S(1)}, bf16[256,1024]{1,0:T(8,128)(2,1)}, u32[]{:S(2)}) copy-start(bf16[256,1024]{1,0:T(8,128)(2,1)} %keys.1) | copy-start | bytes 1572868
  3.1 6.1 %copy-start.7 = (bf16[512,256]{1,0:T(8,128)(2,1)S(1)}, bf16[512,256]{1,0:T(8,128)(2,1)}, u32[]{:S(2)}) copy-start(bf16[512,256]{1,0:T(8,128)(2,1)} %constant.21.clone.forward) | copy-start | bytes 786436
  3.1 26.5 %all-to-all-start = ((bf16[8,768,128]{2,1,0:T(8,128)(2,1)}), bf16[8,768,128]{2,1,0:T(8,128)(2,1)S(1)}, u32[]{:S(2)}, u32[]{:S(2)}) async-start(bf16[8,768,128]{2,1,0:T(8,128)(2,1)} %bitcast.1), calls=%async_computation | async-start | bytes 3145728 | tf_op jit(solution)/shard_map/all_to_all | solution.py:400
  9.5 1.0 %copy-start.2 = (bf16[8,2,256,128]{3,2,1,0:T(8,128)(2,1)}, bf16[8,2,256,128]{3,2,1,0:T(8,128)(2,1)S(1)}, u32[]{:S(2)}) copy-start(bf16[8,2,256,128]{3,2,1,0:T(8,128)(2,1)S(1)} %get-tuple-element.13) | copy-start | bytes 3145732
  30.7 5.5 %collective-permute-start.1 = (bf16[8,256,128]{2,1,0:T(8,128)(2,1)}, bf16[8,256,128]{2,1,0:T(8,128)(2,1)}, u32[]{:S(2)}, u32[]{:S(2)}) collective-permute-start(bf16[8,256,128]{2,1,0:T(8,128)(2,1)} %get-tuple-element.20), channel_id=1, source_target_pairs={{0,8},{8,0},{1,9},{9,1},{2,10},{10,2},{3,11},{11,3},{4,12},{12,4},... | collective-permute-start | bytes 1572872 | tf_op jit(solution)/shard_map/ppermute | solution.py:405
  32.6 3.7 %collective-permute-start = (bf16[8,256,128]{2,1,0:T(8,128)(2,1)}, bf16[8,256,128]{2,1,0:T(8,128)(2,1)S(1)}, u32[]{:S(2)}, u32[]{:S(2)}) collective-permute-start(bf16[8,256,128]{2,1,0:T(8,128)(2,1)} %get-tuple-element.21), channel_id=1, source_target_pairs={{0,8},{8,0},{1,9},{9,1},{2,10},{10,2},{3,11},{11,3},{4,12},{12,4},... | collective-permute-start | bytes 1572872 | tf_op jit(solution)/shard_map/ppermute | solution.py:405
  32.6 18.8 %all-to-all-start.1 = ((bf16[8,512,128]{2,1,0:T(8,128)(2,1)}), bf16[8,512,128]{2,1,0:T(8,128)(2,1)S(1)}, u32[]{:S(2)}, u32[]{:S(2)}) async-start(bf16[8,512,128]{2,1,0:T(8,128)(2,1)} %bitcast.22), calls=%async_computation.1 | async-start | bytes 2097152 | tf_op jit(solution)/shard_map/all_to_all | solution.py:400
  36.3 0.8 %copy-start.5 = (bf16[8,256,128]{2,1,0:T(8,128)(2,1)}, bf16[8,256,128]{2,1,0:T(8,128)(2,1)S(1)}, u32[]{:S(2)}) copy-start(bf16[8,256,128]{2,1,0:T(8,128)(2,1)S(1)} %collective-permute-done.x_other) | copy-start | bytes 1572868
  37.1 1.0 %copy-start.6 = (bf16[8,256,128]{2,1,0:T(8,128)(2,1)S(1)}, bf16[8,256,128]{2,1,0:T(8,128)(2,1)}, u32[]{:S(2)}) copy-start(bf16[8,256,128]{2,1,0:T(8,128)(2,1)} %copy-done.5) | copy-start | bytes 1572868
  45.1 7.8 %copy-start.1 = (bf16[8,256,128]{2,1,0:T(8,128)(2,1)}, bf16[8,256,128]{2,1,0:T(8,128)(2,1)S(1)}, u32[]{:S(2)}) copy-start(bf16[8,256,128]{2,1,0:T(8,128)(2,1)S(1)} %shard_map.97.refs_0_) | copy-start | bytes 1572868
  45.1 6.3 %collective-permute-start.2 = (bf16[8,256,128]{2,1,0:T(8,128)(2,1)S(1)}, bf16[8,256,128]{2,1,0:T(8,128)(2,1)S(1)}, u32[]{:S(2)}, u32[]{:S(2)}) collective-permute-start(bf16[8,256,128]{2,1,0:T(8,128)(2,1)S(1)} %shard_map.97.refs_0_), channel_id=1, source_target_pairs={{0,8},{8,0},{1,9},{9,1},{2,10},{10,2},{3,11},{11,3},{4,12},{12,4},... | collective-permute-start | bytes 1572872 | tf_op jit(solution)/shard_map/ppermute | solution.py:405
  51.5 5.0 %collective-permute-start.3 = (bf16[8,256,128]{2,1,0:T(8,128)(2,1)S(1)}, bf16[8,256,128]{2,1,0:T(8,128)(2,1)S(1)}, u32[]{:S(2)}, u32[]{:S(2)}) collective-permute-start(bf16[8,256,128]{2,1,0:T(8,128)(2,1)S(1)} %slice_bitcast_fusion), channel_id=1, source_target_pairs={{0,8},{8,0},{1,9},{9,1},{2,10},{10,2},{3,11},{11,3},{4,12},{12,4},... | collective-permute-start | bytes 1572872 | tf_op jit(solution)/shard_map/ppermute | solution.py:405
